TPU v7x, 256 devices: a whole 4x4x8 slice. The times are simulated.
256 devices in a mesh: seq: 2 (over core), dp: 8 (over z), island: 16 (over y, x).
Axes of the slice: x: 4, y: 4, z: 8, core: 2. Of those that a mesh axis runs over, the one named last changes fastest.
Arguments:
- layer_input: bfloat16 [16, 8, 256, 8192], P('island', 'dp', 'seq'), may hold values from -6 to 6
- inner_acts: bfloat16 [16, 8, 256, 8192], P('island', 'dp', 'seq'), may hold values from -6 to 6
- out_grad: bfloat16 [16, 8, 256, 8192], P('island', 'dp', 'seq'), may hold values from -6 to 6
- step_sizes: float32 [16, 8, 256, 128], P('island', 'dp', 'seq'), may hold values from 0 to 1.2
- outer_weight: float32 [8192, 256], P(('seq', 'dp')), may hold values from -6 to 6
- island_drift: float32 [16, 8192, 256], P('island', ('seq', 'dp')), may hold values from -6 to 6
- momentum: float32 [8192, 256], P(('seq', 'dp')), may hold values from -6 to 6
Outputs:
- in_grad: bfloat16 [16, 8, 256, 8192], P('island', 'dp', 'seq')
- sel_grad: bfloat16 [16, 8, 256, 256], P('island', 'dp', 'seq')
- new_momentum: float32 [8192, 256], P(('seq', 'dp'))
- new_outer: float32 [8192, 256], P(('seq', 'dp'))
All inputs are finite; a program needn't handle non-finite values.
Results may differ from a plain program's by a relative error of at most 0.007.
Values may be sent and summed in bfloat16 or wider, within the bound.
A program may use at most 192 MiB of HBM per device.

v0:
```python
import math

import jax
import jax.numpy as jnp
from jax import lax
from jax.sharding import PartitionSpec as P

LOCAL_HEADS = 128
HEAD_DIM = 64
STATE = 128


def prefix(part, axis, combine, identity, reverse):
    count = lax.axis_size(axis)
    place = lax.axis_index(axis)
    ahead = count - 1 - place if reverse else place
    gathered = jax.tree.map(lambda a: lax.all_gather(a, axis), part)
    state = jax.tree.map(lambda a, e: jnp.zeros_like(a) + jnp.asarray(e, a.dtype), part, identity)

    def one(lap, state):
        source = count - 1 - lap if reverse else lap
        return combine(
            state, jax.tree.map(lambda a: lax.dynamic_index_in_dim(a, source, 0, False), gathered)
        )

    return lax.fori_loop(0, ahead, one, state)


def block_decays(step_block):
    levels = jnp.cumsum(step_block, axis=0)
    finals = levels[-1]
    entry_decay = jnp.exp(-levels)
    exit_weight = step_block * jnp.exp(levels - finals[None, :])
    return (levels, finals, entry_decay, exit_weight)


def chain_states(earlier, later):
    return (earlier[0] * later[0], later[0][:, None, None] * earlier[1] + later[1])


def local(layer_input, inner_acts, out_grad, step_sizes, outer_weight, island_drift, momentum):
    tokens = layer_input[0, 0]
    inner_block = inner_acts[0, 0]
    grad_block = out_grad[0, 0]
    step_block = step_sizes[0, 0]
    rows_here = step_block.shape[0]
    inv_root = 1.0 / math.sqrt(tokens.shape[1])
    weight_rows = (outer_weight + island_drift[0]).astype(jnp.bfloat16)
    columns = tokens
    sel_sum = jnp.dot(
        columns,
        lax.all_gather(weight_rows, ("seq", "dp"), axis=0, tiled=True),
        preferred_element_type=jnp.float32,
    )
    sel_block = (sel_sum * inv_root).astype(jnp.bfloat16)
    input_map = sel_block[:, :STATE].astype(jnp.float32)
    output_map = sel_block[:, STATE:].astype(jnp.float32)
    levels, finals, entry_decay, exit_weight = block_decays(step_block)
    inner_heads = inner_block.reshape(rows_here, LOCAL_HEADS, HEAD_DIM)
    grad_heads = grad_block.reshape(rows_here, LOCAL_HEADS, HEAD_DIM)
    inner_f = inner_heads.astype(jnp.float32)
    grad_f = grad_heads.astype(jnp.float32)
    inner_weighted = inner_f * exit_weight[:, :, None]
    grad_weighted = grad_f * entry_decay[:, :, None]
    shrink = jnp.exp(-finals)
    produced = jnp.einsum("sn,shp->hnp", input_map, inner_weighted, precision=lax.Precision.HIGHEST)
    received = jnp.einsum("rn,rhp->hnp", output_map, grad_weighted, precision=lax.Precision.HIGHEST)
    ones_head = jnp.ones_like(shrink)
    zero_state = jnp.zeros_like(produced)
    before = prefix((shrink, produced), "seq", chain_states, (ones_head, zero_state), False)
    after = prefix((shrink, received), "seq", chain_states, (ones_head, zero_state), True)
    state_in = before[1]
    adjoint_out = after[1]
    spans = levels.T[:, :, None] - levels.T[:, None, :]
    token_positions = jnp.arange(rows_here)
    lower = token_positions[:, None] >= token_positions[None, :]
    within = jnp.exp(-jnp.where(lower[None, :, :], spans, jnp.inf))
    scores = jnp.einsum("thp,shp->hts", grad_heads, inner_heads, preferred_element_type=jnp.float32)
    mixing = jnp.sum(within * scores * step_block.T[:, None, :], axis=0)
    intersection = jnp.dot(
        sel_block[:, STATE:], sel_block[:, :STATE].T, preferred_element_type=jnp.float32
    )
    d_input = jnp.dot(mixing.T, output_map, precision=lax.Precision.HIGHEST) + jnp.einsum(
        "shp,hnp->sn", inner_weighted, adjoint_out, precision=lax.Precision.HIGHEST
    )
    d_output = jnp.dot(mixing, input_map, precision=lax.Precision.HIGHEST) + jnp.einsum(
        "thp,hnp->tn", grad_weighted, state_in, precision=lax.Precision.HIGHEST
    )
    local_part = jnp.einsum(
        "hrs,rhp->shp", within * intersection[None, :, :], grad_f, precision=lax.Precision.HIGHEST
    )
    carried = jnp.einsum("sn,hnp->shp", input_map, adjoint_out, precision=lax.Precision.HIGHEST)
    in_grad = (
        (step_block[:, :, None] * local_part + exit_weight[:, :, None] * carried)
        .reshape(rows_here, LOCAL_HEADS * HEAD_DIM)
        .astype(jnp.bfloat16)
    )
    sel_grad = jnp.concatenate([d_input, d_output], axis=1).astype(jnp.bfloat16)
    columns = tokens
    weight_grad = lax.psum_scatter(
        jnp.einsum("td,tn->dn", columns, sel_grad, preferred_element_type=jnp.float32),
        ("seq", "dp"),
        scatter_dimension=0,
        tiled=True,
    )
    pseudo = 0.5 * (weight_grad * inv_root) - island_drift[0]
    outer_delta = lax.psum(pseudo, "island") / lax.axis_size("island")
    new_momentum = 0.9 * momentum + outer_delta
    new_outer = outer_weight - 0.7 * (outer_delta + 0.9 * new_momentum)
    return (
        in_grad.reshape(1, 1, rows_here, LOCAL_HEADS * HEAD_DIM),
        sel_grad.reshape(1, 1, rows_here, 2 * STATE),
        new_momentum,
        new_outer,
    )


def solution(mesh):
    placed = (
        P("island", "dp", "seq", None),
        P("island", "dp", "seq", None),
        P("island", "dp", "seq", None),
        P("island", "dp", "seq", None),
        P(("seq", "dp"), None),
        P("island", ("seq", "dp"), None),
        P(("seq", "dp"), None),
    )
    return jax.shard_map(
        local,
        mesh=mesh,
        in_specs=placed,
        out_specs=(
            P("island", "dp", "seq", None),
            P("island", "dp", "seq", None),
            P(("seq", "dp"), None),
            P(("seq", "dp"), None),
        ),
        check_vma=False,
    )
```

profile of v0, /device:TPU:6, one launch (start us, length us, event | category | flops | bytes accessed | tf_op | source)
XLA Modules:
  0.0 370.5 jit_solution(6383969918774315275)
XLA Ops:
  7.2 1.4 copy.72
  8.6 1.4 copy.73
  10.1 0.9 fusion.33
  11.0 1.0 reduce_window_sum.11
  12.1 0.9 exponential_multiply_fusion
  12.9 0.1 copy.76
  13.0 4.1 %copy.74 = bf16[1,1,128,8192]{2,3,1,0:T(8,128)(2,1)} copy(bf16[1,1,128,8192]{3,2,1,0:T(8,128)(2,1)} %param.13) | data formatting | bytes 4194304 | tf_op args[2]
  17.1 4.2 %convert_multiply_fusion.1 = f32[128,128,64]{0,2,1:T(8,128)} fusion(bf16[128,128,64]{0,2,1:T(8,128)(2,1)} %bitcast.87, f32[128,128]{0,1:T(8,128)S(1)} %copy.76), kind=kLoop, calls=%fused_computation.19 | loop fusion | flops 2097152 | bytes 6356992 | tf_op jit(solution)/shard_map/mul | solution.py:64
  21.4 34.8 %all-gather.7.cloned.1.call-done = bf16[8192,256]{0,1:T(8,128)(2,1)} async-done(((bf16[512,256]{0,1:T(8,128)(2,1)}), bf16[8192,256]{0,1:T(8,128)(2,1)}) %all-gather.7.cloned.1.call-update) | async-done | bytes 4194320 | tf_op jit(solution)/shard_map/all_gather | solution.py:52
  56.2 3.6 fusion.28
  59.8 5.9 %fusion.13 = f32[128,128,64]{1,0,2:T(8,128)} fusion(f32[128,128,64]{0,2,1:T(8,128)S(1)} %copy-done.1, bf16[128,256]{0,1:T(8,128)(2,1)S(1)} %fusion.28), kind=kOutput, calls=%fused_computation.25 | convolution fusion | flops 1610612736 | bytes 8421376 | tf_op jit(solution)/shard_map/rn,rhp->hnp/dot_general | solution.py:67
  65.8 0.1 copy.75
  65.9 4.1 %copy.83 = bf16[1,1,128,8192]{2,3,1,0:T(8,128)(2,1)} copy(bf16[1,1,128,8192]{3,2,1,0:T(8,128)(2,1)} %param.12) | data formatting | bytes 4194304 | tf_op args[1]
  70.0 2.2 convert_multiply_fusion
  72.2 6.0 %fusion.16 = f32[128,128,64]{1,0,2:T(8,128)} fusion(f32[128,128,64]{0,2,1:T(8,128)S(1)} %convert_multiply_fusion, bf16[128,256]{0,1:T(8,128)(2,1)S(1)} %fusion.28), kind=kOutput, calls=%fused_computation.26 | convolution fusion | flops 1610612736 | bytes 8421376 | tf_op jit(solution)/shard_map/sn,shp->hnp/dot_general | solution.py:66
  78.3 0.1 copy.70
  78.4 0.7 copy-done.6
  79.1 0.1 copy.84
  79.2 1.8 all-gather.2
  81.0 5.5 %multiply_reduce_fusion = f32[128,128]{1,0:T(8,128)S(1)} fusion(f32[128,128]{1,0:T(8,128)S(1)} %copy.84, f32[128,128]{1,0:T(8,128)S(1)} %copy.70, pred[128,128]{1,0:T(8,128)(4,1)S(1)} %iota_compare_fusion, bf16[128,128,64]{0,2,1:T(8,128)(2,1)} %bitcast.88, bf16[128,128,64]{0,2,1:T(8,128)(2,1)} %bitcast.92), kind=kOutput, calls=%fused_computation.7 | convolution fusion | flops 281001984 | bytes 4407296 | tf_op jit(solution)/shard_map/thp,shp->hts/dot_general | solution.py:78
  86.5 3.1 all-gather.9.cloned.1.call-done
  89.7 4.3 %broadcast_in_dim.16.clone = f32[128,128,64]{2,1,0:T(8,128)} broadcast(f32[]{:T(128)} %constant.62.clone.1), dimensions={} | broadcast | bytes 4194308 | tf_op jit(solution)/shard_map/broadcast_in_dim | solution.py:69
  94.0 24.3 %while.26 = (s32[]{:T(128)}, f32[128,128,64]{2,1,0:T(8,128)}, s32[]{:T(128)}, f32[2,128]{1,0:T(2,128)S(1)}, f32[2,128,128,64]{2,1,0,3:T(8,128)}, /*index=5*/s32[]{:T(128)}, s32[]{:T(128)}, s32[]{:T(128)}) while((s32[]{:T(128)}, f32[128,128,64]{2,1,0:T(8,128)}, s32[]{:T(128)}, f32[2,128]{1,0:T(2,128)S(1)}, f32[2,128,128,64]{2,1,0,3:T(8,128)}, ...), condition=%wide.region_2.3_spmd, body=%wide.region_1.2_spmd.sunk | while | flops 2097158 | bytes 29361804 | solution.py:26
  94.0 4.7 %constant_dynamic-slice_fusion.4 = f32[1,128,128,64]{2,1,0,3:T(8,128)} fusion(f32[2,128,128,64]{2,1,0,3:T(8,128)} %get-tuple-element.286, s32[]{:T(128)S(6)} %select_n.30), kind=kLoop, calls=%fused_computation.2.clone.1 | loop fusion | bytes 8388612 | tf_op jit(solution)/shard_map/while/body/jit(dynamic_index_in_dim)/dynamic_slice | solution.py:23
  98.6 7.0 %copy.118 = f32[1,128,128,64]{3,2,1,0:T(8,128)} copy(f32[1,128,128,64]{2,1,0,3:T(8,128)} %constant_dynamic-slice_fusion.4) | data formatting | bytes 8388608 | tf_op jit(solution)/shard_map/while/body/jit(dynamic_index_in_dim)/dynamic_slice | solution.py:23
  105.6 12.7 %bitcast_add_fusion.5 = f32[128,128,64]{2,1,0:T(8,128)} fusion(f32[1,128,128,64]{3,2,1,0:T(8,128)} %copy.118, f32[128,128,64]{2,1,0:T(8,128)} %get-tuple-element.275, f32[128]{0:T(128)S(1)} %dynamic-slice_bitcast_fusion.4), kind=kLoop, calls=%fused_computation.clone.1 | loop fusion | flops 2097152 | bytes 12583424 | tf_op jit(solution)/shard_map/while/body/add | solution.py:38
  118.3 10.1 %convolution_bitcast_fusion.2 = f32[128,128]{0,1:T(8,128)S(1)} fusion(f32[128,128,64]{2,1,0:T(8,128)} %get-tuple-element.132, bf16[128,128,64]{0,2,1:T(8,128)(2,1)} %bitcast.93, f32[128,128]{0,1:T(8,128)S(1)} %copy.75), kind=kOutput, calls=%fused_computation.35 | convolution fusion | flops 1612709888 | bytes 6422528 | tf_op jit(solution)/shard_map/shp,hnp->sn/dot_general | solution.py:83
  128.4 4.3 %broadcast_in_dim.16.clone.1 = f32[128,128,64]{2,1,0:T(8,128)} broadcast(f32[]{:T(128)} %constant.62.clone.1), dimensions={} | broadcast | bytes 4194308 | tf_op jit(solution)/shard_map/broadcast_in_dim | solution.py:69
  132.7 0.8 copy-done.9
  133.6 10.1 %convolution_bitcast_fusion.1 = f32[128,128]{0,1:T(8,128)S(1)} fusion(f32[128,128,64]{2,1,0:T(8,128)} %get-tuple-element.133, bf16[128,128,64]{0,2,1:T(8,128)(2,1)} %bitcast.89, f32[128,128]{0,1:T(8,128)S(1)} %copy-done.9), kind=kOutput, calls=%fused_computation.33 | convolution fusion | flops 1612709888 | bytes 6422528 | tf_op jit(solution)/shard_map/thp,hnp->tn/dot_general | solution.py:86
  143.7 0.2 fusion.31
  143.8 0.2 fusion.32
  144.1 4.5 %convolution_bitcast_fusion = f32[8192,256]{0,1:T(8,128)} fusion(bf16[1,1,128,8192]{3,2,1,0:T(8,128)(2,1)S(1)} %copy-done, bf16[128,128]{0,1:T(8,128)(2,1)S(1)} %fusion.32, bf16[128,128]{0,1:T(8,128)(2,1)S(1)} %fusion.31), kind=kOutput, calls=%fused_computation.6 | convolution fusion | flops 537001984 | bytes 10551296 | tf_op jit(solution)/shard_map/td,tn->dn/dot_general | solution.py:101
  148.6 0.3 all-reduce.2.cloned.1.call-start
  148.8 0.5 copy-done.7
  149.4 0.1 copy.69
  149.5 1.2 copy.90
  150.7 0.2 fusion.42
  150.9 8.3 %fusion = f32[128,128,64]{1,2,0:T(8,128)} fusion(bf16[128,128,64]{0,2,1:T(8,128)(2,1)} %bitcast.90, f32[128,128]{1,0:T(8,128)S(1)} %fusion.42, f32[128,128]{1,0:T(8,128)S(1)} %copy.70, pred[128,128]{1,0:T(8,128)(4,1)S(1)} %iota_compare_fusion), kind=kOutput, calls=%fused_computation.8 | convolution fusion | flops 1619001344 | bytes 6438912 | tf_op jit(solution)/shard_map/hrs,rhp->shp/dot_general | solution.py:89
  159.3 0.7 copy.93
  160.0 100.3 %reduce-scatter.2.cloned.1.call-done = f32[512,256]{0,1:T(8,128)} async-done(((f32[8192,256]{0,1:T(8,128)}), f32[512,256]{0,1:T(8,128)}) %reduce-scatter.2.cloned.1.call-update) | async-done | bytes 524304 | tf_op jit(solution)/shard_map/reduce_scatter | solution.py:100
  260.3 1.9 bitcast_subtract_fusion
  262.3 12.6 %fusion.3 = bf16[128,128,64]{0,2,1:T(8,128)(2,1)} fusion(f32[128,128,64]{1,2,0:T(8,128)} %fusion, f32[128,128,64]{2,1,0:T(8,128)} %get-tuple-element.132, f32[128,128]{0,1:T(8,128)S(1)} %copy.75, f32[128,128]{0,1:T(8,128)S(1)} %copy.69, bf16[128,256]{0,1:T(8,128)(2,1)S(1)} %fusion.28), kind=kOutput, calls=%fused_computation.13 | convolution fusion | flops 1614807040 | bytes 10649600 | tf_op jit(solution)/shard_map/sn,hnp->shp/dot_general | solution.py:92
  274.9 4.1 %copy.92 = bf16[1,1,128,8192]{3,2,1,0:T(8,128)(2,1)} copy(bf16[1,1,128,8192]{2,3,1,0:T(8,128)(2,1)} %bitcast.94) | data formatting | bytes 4194304
  279.0 78.7 %all-reduce.2.cloned.1.call-done = f32[512,256]{0,1:T(8,128)} async-done(((f32[512,256]{0,1:T(8,128)}), f32[512,256]{0,1:T(8,128)}) %all-reduce.2.cloned.1.call-update) | async-done | bytes 524304 | tf_op jit(solution)/shard_map/psum | solution.py:107
  357.7 2.2 multiply_subtract_fusion
  359.9 2.0 copy.94
  361.9 2.0 copy.95
  (32 shorter events, 0.3 us)
Async XLA Ops:
  7.2 49.0 %copy-start = (bf16[1,1,128,8192]{3,2,1,0:T(8,128)(2,1)S(1)}, bf16[1,1,128,8192]{3,2,1,0:T(8,128)(2,1)}, u32[]{:S(2)}) copy-start(bf16[1,1,128,8192]{3,2,1,0:T(8,128)(2,1)} %param.11) | copy-start | bytes 6291460
  7.2 49.0 %all-gather.7.cloned.1.call-start = ((), (), s32[]{:S(2)}) async-start(), calls=%async_computation.1 | async-start | bytes 4456448 | tf_op jit(solution)/shard_map/all_gather | solution.py:52
  8.6 12.8 %copy-start.4 = (f32[1,512,256]{1,2,0:T(8,128)}, f32[1,512,256]{1,2,0:T(8,128)S(1)}, u32[]{:S(2)}) copy-start(f32[1,512,256]{1,2,0:T(8,128)S(1)} %copy.72) | copy-start | bytes 1572868
  10.1 11.3 %copy-start.2 = (f32[512,256]{0,1:T(8,128)}, f32[512,256]{0,1:T(8,128)S(1)}, u32[]{:S(2)}) copy-start(f32[512,256]{0,1:T(8,128)S(1)} %copy.73) | copy-start | bytes 1572868
  11.0 78.7 %all-gather.9.cloned.1.call-start = ((), (), s32[]{:S(2)}) async-start(), calls=%async_computation.4 | async-start | bytes 12582912 | tf_op jit(solution)/shard_map/all_gather | solution.py:17
  13.0 8.3 %copy-start.8 = (f32[128,128]{0,1:T(8,128)}, f32[128,128]{0,1:T(8,128)S(1)}, u32[]{:S(2)}) copy-start(f32[128,128]{0,1:T(8,128)S(1)} %copy.76) | copy-start | bytes 196612
  56.2 3.6 copy-start.1
  65.7 62.7 %all-gather.11.cloned.1.call-start = ((), (), s32[]{:S(2)}) async-start(), calls=%async_computation.5 | async-start | bytes 12582912 | tf_op jit(solution)/shard_map/all_gather | solution.py:17
  78.3 0.9 copy-start.6
  78.3 182.0 %reduce-scatter.2.cloned.1.call-start = ((), (), s32[]{:S(2)}) async-start(), calls=%async_computation.2 | async-start | bytes 8912896 | tf_op jit(solution)/shard_map/reduce_scatter | solution.py:100
  132.7 0.8 copy-start.9
  148.6 0.8 copy-start.7
  148.6 209.1 %all-reduce.2.cloned.1.call-start = ((), (), s32[]{:S(2)}) async-start(), calls=%async_computation.3 | async-start | bytes 1048576 | tf_op jit(solution)/shard_map/psum | solution.py:107
  150.9 109.4 %copy-start.5 = (f32[1,512,256]{1,2,0:T(8,128)S(1)}, f32[1,512,256]{1,2,0:T(8,128)}, u32[]{:S(2)}) copy-start(f32[1,512,256]{1,2,0:T(8,128)} %copy-done.4) | copy-start | bytes 1572868
  274.9 82.8 %copy-start.3 = (f32[512,256]{0,1:T(8,128)S(1)}, f32[512,256]{0,1:T(8,128)}, u32[]{:S(2)}) copy-start(f32[512,256]{0,1:T(8,128)} %copy-done.2) | copy-start | bytes 1572868
Sparse Core Ops, SparseCore 0:
  11.1 45.0 all-gather.6
  65.9 23.7 all-gather.8
  91.5 26.4 all-gather.10
  148.7 111.5 reduce-scatter.1
  263.9 93.7 all-reduce.1
where the time goes:
time: 372 us; the launch traced here: 371 us
  waiting for transfers between devices  217 us (58%)
  matrix products  67.3 us (18%)
  local copies, waits for them, and re-layouts  44 us (12%)
  other arithmetic  26.1 us (7%)
  between operations  14 us (4%)
    reduce_scatter x1, waiting for transfers between devices, local(): lax.psum_scatter(jnp.einsum('td,tn->dn', columns, sel_grad, preferred_ele...  100 us
    psum x1, waiting for transfers between devices, local(): outer_delta = lax.psum(pseudo, 'island') / lax.axis_size('island')  78.7 us
    all_gather x1, waiting for transfers between devices, local(): lax.all_gather(weight_rows, ('seq', 'dp'), axis=0, tiled=True)  34.8 us
    unnamed x29, local copies, waits for them, and re-layouts  23.3 us
    add x1, other arithmetic, chain_states(): later[0][:, None, None] * earlier[1] + later[1]  12.7 us
    dot_general x1, matrix products, local(): jnp.einsum('sn,hnp->shp', input_map, adjoint_out, precision=lax.Precision...  12.6 us
    dynamic_slice x2, local copies, waits for them, and re-layouts, one(): lax.dynamic_index_in_dim(a, source, 0, False)  11.6 us
    dot_general x1, matrix products, local(): jnp.einsum('thp,hnp->tn', grad_weighted, state_in, precision=lax.Precisio...  10.1 us
  transfers between devices with their start and end apart: 5, of which 4 were waited for; matrix products, arithmetic and copies ran while one was open for 26% of the time, Pallas kernels for 0%

commit v1 on v0

v1 whole, which is shorter than its diff:
```python
import functools
import math

import jax
import jax.numpy as jnp
from jax import lax
from jax.experimental import pallas as pl
from jax.experimental.pallas import tpu as pltpu
from jax.sharding import PartitionSpec as P

MESH = pl.DeviceIdType.MESH
BF = jnp.bfloat16
F32 = jnp.float32
HEADS = 128
T = 128
NZ = 8
NQ = 4
VMEM_LIMIT = 50 * 1024 * 1024


def dot(a, b, ca=1, cb=0):
    return lax.dot_general(a, b, (((ca,), (cb,)), ((), ())), preferred_element_type=F32)


def remote(src, dst, send, recv, device):
    return pltpu.make_async_remote_copy(
        src_ref=src, dst_ref=dst, send_sem=send, recv_sem=recv, device_id=device, device_id_type=MESH
    )


def kernel(
    x_hbm, ia_hbm, dy_hbm, dt_hbm, ow_hbm, dr_hbm,
    ig_hbm, sg_hbm, delta_hbm,
    ow, dr, dt, ia, dy, wg, xs, xr, xt, ds16, dr16,
    lq, lt, mixacc, ew, pw, ewx, gw, e_all, ig, mb, mt2, m2,
    psel, prem, sel, sall, gf, gs, r2, t2, t2b, r3, dl,
    loc, ring_s, ring_r, pair_s, pair_r, xr_s, xr_r, dr_s, dr_r,
    s_s, s_r, p_s, p_r, z_s, z_r, a_s, a_r, b_s, b_r, outs,
):
    s = lax.axis_index("seq")
    z = lax.axis_index("dp")
    isl = lax.axis_index("island")
    y = isl // 4
    x = isl % 4
    p1 = x + s * (y - x)
    p2 = y + s * (x - y)
    base1 = (1 - s) * 4 * y + s * x
    mul1 = 1 + 3 * s
    base2 = (1 - s) * x + s * 4 * y
    mul2 = 4 - 3 * s

    def first(k):
        return {"seq": s, "dp": z, "island": base1 + mul1 * ((p1 + k) % 4)}

    def second(k):
        return {"seq": s, "dp": z, "island": base2 + mul2 * ((p2 + k) % 4)}

    def along(k):
        return {"seq": s, "dp": (z + k) % 8, "island": isl}

    partner = {"seq": 1 - s, "dp": z, "island": isl}

    c_ow = pltpu.make_async_copy(ow_hbm, ow, loc.at[0])
    c_dr = pltpu.make_async_copy(dr_hbm, dr, loc.at[1])
    c_dt = pltpu.make_async_copy(dt_hbm, dt, loc.at[2])
    c_ia = pltpu.make_async_copy(ia_hbm, ia, loc.at[3])
    c_dy = pltpu.make_async_copy(dy_hbm, dy, loc.at[4])
    for c in (c_ow, c_dr, c_dt, c_dy, c_ia):
        c.start()

    def load_x(c, carry):
        col = pl.multiple_of(s * 4096 + c * 128, 128)
        pltpu.make_async_copy(
            x_hbm.at[:, pl.ds(col, 128)], xs.at[c % 4, c // 4, pl.ds(pl.multiple_of(s * T, T), T)], loc.at[5]
        ).start()
        return carry

    lax.fori_loop(0, 32, load_x, 0)

    barrier = pltpu.get_barrier_semaphore()
    peers = [partner] + [along(k) for k in range(1, 8)] + [first(k) for k in range(1, 4)] + [second(k) for k in range(1, 4)]
    for d in peers:
        pl.semaphore_signal(barrier, inc=1, device_id=d, device_id_type=MESH)

    c_ow.wait()
    c_dr.wait()
    wg[z] = (ow[...] + dr[...]).astype(BF)
    for q in range(4):
        ds16[q] = dr[pl.ds(q * 128, 128), :].astype(BF)

    pl.semaphore_wait(barrier, len(peers))

    def right(j, zb, half):
        at = wg.at[zb, pl.ds(pl.multiple_of(half * 256, 256), 256)]
        return remote(at, at, ring_s.at[0, j], ring_r.at[0, j], along(1))

    def left(j, zb, half):
        at = wg.at[zb, pl.ds(pl.multiple_of(half * 256, 256), 256)]
        return remote(at, at, ring_s.at[1, j], ring_r.at[1, j], along(7))

    right(0, z, 0).start()
    left(0, z, 1).start()
    right(1, z, 1).start()
    left(1, z, 0).start()

    def send_x(c, carry):
        col = pl.multiple_of((1 - s) * 4096 + c * 128, 128)
        remote(
            x_hbm.at[:, pl.ds(col, 128)], xs.at[c % 4, c // 4, pl.ds(pl.multiple_of(s * T, T), T)],
            pair_s.at[0], pair_r.at[0], partner,
        ).start()
        return carry

    lax.fori_loop(0, 32, send_x, 0)

    c_dt.wait()
    rows = lax.broadcasted_iota(jnp.int32, (T, T), 0)
    cols = lax.broadcasted_iota(jnp.int32, (T, T), 1)
    tri = (rows >= cols).astype(F32)
    steps = dt[...]
    levels = lax.dot_general(
        tri, steps, (((1,), (0,)), ((), ())), precision=lax.Precision.HIGHEST, preferred_element_type=F32
    )
    finals = levels[T - 1 : T, :]
    logs = jnp.where(steps > 0.0, jnp.log(jnp.where(steps > 0.0, steps, 1.0)), -1e30)
    lq[...] = levels + logs
    lt[...] = levels.T
    first_core = s == 0
    factor = jnp.exp(jnp.where(first_core, (levels - finals) + logs, -levels))
    hi = factor.astype(BF)
    ew[:, 0:T] = hi
    ew[:, T : 2 * T] = (factor - hi.astype(F32)).astype(BF)
    c_ia.wait()
    c_dy.wait()

    def widen(c, carry):
        wide = 512
        kk = lax.broadcasted_iota(jnp.int32, (2 * T, wide), 0)
        ll = lax.broadcasted_iota(jnp.int32, (2 * T, wide), 1)
        spread = ((kk % T) == c * 8 + ll // 64).astype(F32).astype(BF)
        fac = dot(ew[...], spread)
        off = pl.ds(pl.multiple_of(c * wide, wide), wide)
        ewx[:, off] = fac.astype(BF)

        @pl.when(s == 0)
        def _():
            pw[:, off] = (ia[:, off].astype(F32) * fac).astype(BF)

        @pl.when(s == 1)
        def _():
            gw[:, off] = (dy[:, off].astype(F32) * fac).astype(BF)

        return carry

    lax.fori_loop(0, 16, widen, 0)

    c_gw = remote(gw, gw, pair_s.at[1], pair_r.at[1], partner)

    @pl.when(s == 1)
    def _():
        c_gw.start()

    own_x = xs.at[:, :, pl.ds(pl.multiple_of(s * T, T), T)]
    pltpu.make_async_copy(own_x, own_x, loc.at[5]).wait()
    other_x = xs.at[:, :, pl.ds(pl.multiple_of((1 - s) * T, T), T)]
    remote(own_x, other_x, pair_s.at[0], pair_r.at[0], partner).wait_recv()
    for k in range(1, 4):
        remote(xs.at[(p1 + k) % 4], xr.at[k - 1], xr_s.at[k - 1], xr_r.at[k - 1], first(k)).start()
        remote(ds16.at[(p1 + k) % 4], dr16.at[k - 1], dr_s.at[k - 1], dr_r.at[k - 1], first(k)).start()

    mixacc[...] = jnp.zeros((T, T), F32)
    low = lax.broadcasted_iota(jnp.int32, (T, T), 1) < 64
    keep = rows <= cols
    none = jnp.zeros((T, T), BF)

    def group(g):
        shifted = pltpu.roll(lq[...], (128 - 8 * g) % 128, 1)
        lrow = lt[pl.ds(pl.multiple_of(8 * g, 8), 8), :]
        mix = mixacc[...]
        for pair in range(4):
            off = pl.ds(pl.multiple_of(g * 512 + pair * 128, 128), 128)
            xp = ia[:, off]
            both = jnp.concatenate([jnp.where(low, xp, none), jnp.where(low, none, xp)], axis=0)
            scores = dot(both, dy[:, off], 1, 1)
            for u in range(2):
                c = 2 * pair + u
                e = jnp.where(keep, jnp.exp(shifted[:, c : c + 1] - lrow[c : c + 1, :]), 0.0)
                mix = mix + e * scores[u * T : (u + 1) * T, :]
                e_all[g * 8 + c] = e.astype(BF)
        mixacc[...] = mix

    def partial_sel(zb, half):
        a = jnp.concatenate([xs[2 * half, zb], xs[2 * half + 1, zb]], axis=1)
        return dot(a, wg[zb, pl.ds(pl.multiple_of(half * 256, 256), 256), :])

    psel[...] = partial_sel(z, 0) + partial_sel(z, 1)
    group(14)
    group(15)

    def event(j, carry):
        k = j // 2 + 1
        hr = j % 2
        hl = 1 - hr
        zr = (z - k + 8) % 8
        zl = (z + k) % 8
        right(j, zr, hr).wait_recv()

        @pl.when(j < 5)
        def _():
            right(j + 2, zr, hr).start()

        left(j, zl, hl).wait_recv()

        @pl.when(j < 5)
        def _():
            left(j + 2, zl, hl).start()

        psel[...] += partial_sel(zr, hr) + partial_sel(zl, hl)

        @pl.when(j < 6)
        def _():
            group(2 * j)
            group(2 * j + 1)

        return carry

    group(12)
    group(13)
    lax.fori_loop(0, 7, event, 0)

    c_psel = remote(psel, prem, pair_s.at[2], pair_r.at[2], partner)
    c_psel.start()

    c_mb0 = remote(mb.at[pl.ds(0, 2)], mb.at[pl.ds(0, 2)], pair_s.at[3], pair_r.at[3], partner)
    c_mb1 = remote(mb.at[2], mb.at[2], pair_s.at[4], pair_r.at[4], partner)

    @pl.when(s == 0)
    def _():
        c_gw.wait_recv()
        mb[0] = mixacc[...]
        mb[1] = dot(pw[...], gw[...], 1, 1)
        c_mb0.start()
        c_mb1.wait_recv()

    @pl.when(s == 1)
    def _():
        mb[2] = mixacc[...]
        c_mb1.start()
        c_mb0.wait_recv()

    mt = jnp.concatenate(
        [jnp.concatenate([mb[0], mb[1]], axis=1), jnp.concatenate([jnp.zeros((T, T), F32), mb[2]], axis=1)], axis=0
    )
    mth = mt.astype(BF)
    mt2[0] = mth
    mt2[1] = (mt - mth.astype(F32)).astype(BF)
    m = mt.T
    mh = m.astype(BF)
    m2[0] = mh
    m2[1] = (m - mh.astype(F32)).astype(BF)

    def turn_own(zb, carry):
        xt[zb, :, 0:256] = xs[p1, zb].T
        return carry

    lax.fori_loop(0, 8, turn_own, 0)
    for k in range(1, 4):
        remote(xs.at[(p1 + k) % 4], xr.at[k - 1], xr_s.at[k - 1], xr_r.at[k - 1], first(k)).wait_recv()

        def turn(zb, carry):
            xt[zb, :, k * 256 : (k + 1) * 256] = xr[k - 1, zb].T
            return carry

        lax.fori_loop(0, 8, turn, 0)
        remote(ds16.at[(p1 + k) % 4], dr16.at[k - 1], dr_s.at[k - 1], dr_r.at[k - 1], first(k)).wait_recv()

    c_psel.wait_recv()
    sel[...] = ((psel[...] + prem[...]) * (1.0 / math.sqrt(8192.0))).astype(BF)
    bmap = sel[:, 0:T]
    cmap = sel[:, T : 2 * T]
    d_in = dot(mt2[0], cmap) + dot(mt2[1], cmap)
    d_out = dot(m2[0], bmap) + dot(m2[1], bmap)
    sall[0] = jnp.concatenate([d_in, d_out], axis=1).astype(BF)
    for k in range(1, 4):
        remote(sall.at[0], sall.at[k], s_s.at[k - 1], s_r.at[k - 1], first(k)).start()
    c_sg = pltpu.make_async_copy(sall.at[0, pl.ds(pl.multiple_of(s * T, T), T)], sg_hbm, outs.at[0])
    c_sg.start()

    mine = pl.ds(pl.multiple_of(s * T, T), T)
    inter = dot(sel[mine, 0:T], sel[mine, T : 2 * T], 1, 1).astype(BF)
    across = (dot(sel[0:T, 0:T], sel[T : 2 * T, T : 2 * T], 1, 1) * (1 - s).astype(F32)).astype(BF)

    def grads(start, stop):
        def one(j, carry):
            off = pl.ds(pl.multiple_of(j * 128, 128), 128)
            dp = dy[:, off]
            lhs = jnp.concatenate([e_all[2 * j] * inter, e_all[2 * j + 1] * inter], axis=1)
            rhs = jnp.concatenate([jnp.where(low, dp, none), jnp.where(low, none, dp)], axis=0)
            out = dot(lhs, rhs) + ewx[:, off].astype(F32) * dot(across, gw[:, off])
            ig[:, off] = out.astype(BF)
            return carry

        lax.fori_loop(start, stop, one, 0)

    grads(0, 24)

    for k in range(1, 4):
        remote(sall.at[0], sall.at[k], s_s.at[k - 1], s_r.at[k - 1], first(k)).wait_recv()

    scale = 0.5 / math.sqrt(8192.0)

    def weight(zb, carry):
        gf[zb] = dot(xt[zb], sall[...].reshape(1024, 256)) * scale
        return carry

    lax.fori_loop(0, 8, weight, 0)
    drift = dr[pl.ds(pl.multiple_of(p1 * 128, 128), 128), :]
    for k in range(3):
        drift = drift + dr16[k].astype(F32)
    gf[z] = gf[z] - drift
    for q in range(4):
        gs[q] = gf[:, q * 32 : (q + 1) * 32, :].astype(BF)
    for k in range(1, 4):
        remote(gs.at[(p2 + k) % 4], r2.at[k - 1], p_s.at[k - 1], p_r.at[k - 1], second(k)).start()
    grads(24, 40)
    total = gf[:, pl.ds(pl.multiple_of(p2 * 32, 32), 32), :]
    for k in range(1, 4):
        remote(gs.at[(p2 + k) % 4], r2.at[k - 1], p_s.at[k - 1], p_r.at[k - 1], second(k)).wait_recv()
        total = total + r2[k - 1].astype(F32)
    t2[...] = total
    t2b[...] = total.astype(BF)
    for k in range(1, 8):
        remote(t2b.at[(z + k) % 8], r3.at[k - 1], z_s.at[k - 1], z_r.at[k - 1], along(k)).start()
    grads(40, 52)
    part = t2[z]
    for k in range(1, 8):
        remote(t2b.at[(z + k) % 8], r3.at[k - 1], z_s.at[k - 1], z_r.at[k - 1], along(k)).wait_recv()
        part = part + r3[k - 1].astype(F32)
    dl[p1, p2] = (part * (1.0 / 16.0)).astype(BF)
    for k in range(1, 4):
        remote(dl.at[p1, p2], dl.at[p1, p2], a_s.at[k - 1], a_r.at[k - 1], second(k)).start()
    grads(52, 58)
    for k in range(1, 4):
        at = dl.at[p1, (p2 + 4 - k) % 4]
        remote(at, at, a_s.at[k - 1], a_r.at[k - 1], second(k)).wait_recv()
    for k in range(1, 4):
        remote(dl.at[p1], dl.at[p1], b_s.at[k - 1], b_r.at[k - 1], first(k)).start()
    grads(58, 64)
    c_ig = pltpu.make_async_copy(ig, ig_hbm, outs.at[1])
    c_ig.start()
    for k in range(1, 4):
        at = dl.at[(p1 + 4 - k) % 4]
        remote(at, at, b_s.at[k - 1], b_r.at[k - 1], first(k)).wait_recv()
    c_delta = pltpu.make_async_copy(dl, delta_hbm, outs.at[2])
    c_delta.start()

    def drain(j, carry):
        right(j, z, 0).wait_send()
        left(j, z, 0).wait_send()
        return carry

    lax.fori_loop(0, 7, drain, 0)
    remote(own_x, other_x, pair_s.at[0], pair_r.at[0], partner).wait_send()
    c_psel.wait_send()

    @pl.when(s == 0)
    def _():
        c_mb0.wait_send()

    @pl.when(s == 1)
    def _():
        c_gw.wait_send()
        c_mb1.wait_send()

    for k in range(1, 4):
        remote(xs.at[0], xr.at[k - 1], xr_s.at[k - 1], xr_r.at[k - 1], first(k)).wait_send()
        remote(ds16.at[0], dr16.at[k - 1], dr_s.at[k - 1], dr_r.at[k - 1], first(k)).wait_send()
        remote(sall.at[0], sall.at[k], s_s.at[k - 1], s_r.at[k - 1], first(k)).wait_send()
        remote(gs.at[0], r2.at[k - 1], p_s.at[k - 1], p_r.at[k - 1], second(k)).wait_send()
        remote(dl.at[p1, p2], dl.at[p1, p2], a_s.at[k - 1], a_r.at[k - 1], second(k)).wait_send()
        remote(dl.at[p1], dl.at[p1], b_s.at[k - 1], b_r.at[k - 1], first(k)).wait_send()
    for k in range(1, 8):
        remote(t2b.at[0], r3.at[k - 1], z_s.at[k - 1], z_r.at[k - 1], along(k)).wait_send()
    c_sg.wait()
    c_ig.wait()
    c_delta.wait()


def local(layer_input, inner_acts, out_grad, step_sizes, outer_weight, island_drift, momentum):
    anyspec = pl.BlockSpec(memory_space=pl.ANY)
    dma = pltpu.SemaphoreType.DMA
    vm = pltpu.VMEM
    in_grad, sel_grad, delta = pl.pallas_call(
        kernel,
        out_shape=(
            jax.ShapeDtypeStruct((T, 8192), BF),
            jax.ShapeDtypeStruct((T, 256), BF),
            jax.ShapeDtypeStruct((4, 4, 32, 256), BF),
        ),
        in_specs=[anyspec] * 6,
        out_specs=(anyspec, anyspec, anyspec),
        scratch_shapes=[
            vm((512, 256), F32),
            vm((512, 256), F32),
            vm((T, HEADS), F32),
            vm((T, 8192), BF),
            vm((T, 8192), BF),
            vm((8, 512, 256), BF),
            vm((4, 8, 256, 128), BF),
            vm((3, 8, 256, 128), BF),
            vm((8, 128, 1024), BF),
            vm((4, 128, 256), BF),
            vm((3, 128, 256), BF),
            vm((T, HEADS), F32),
            vm((HEADS, T), F32),
            vm((T, T), F32),
            vm((T, 2 * T), BF),
            vm((T, 8192), BF),
            vm((T, 8192), BF),
            vm((T, 8192), BF),
            vm((HEADS, T, T), BF),
            vm((T, 8192), BF),
            vm((3, T, T), F32),
            vm((2, 256, 256), BF),
            vm((2, 256, 256), BF),
            vm((256, 256), F32),
            vm((256, 256), F32),
            vm((256, 256), BF),
            vm((4, 256, 256), BF),
            vm((8, 128, 256), F32),
            vm((4, 8, 32, 256), BF),
            vm((3, 8, 32, 256), BF),
            vm((8, 32, 256), F32),
            vm((8, 32, 256), BF),
            vm((7, 32, 256), BF),
            vm((4, 4, 32, 256), BF),
            dma((6,)),
            dma((2, 7)),
            dma((2, 7)),
            dma((5,)),
            dma((5,)),
            dma((3,)), dma((3,)),
            dma((3,)), dma((3,)),
            dma((3,)), dma((3,)),
            dma((3,)), dma((3,)),
            dma((7,)), dma((7,)),
            dma((3,)), dma((3,)),
            dma((3,)), dma((3,)),
            dma((3,)),
        ],
        compiler_params=pltpu.CompilerParams(
            collective_id=0, has_side_effects=True, vmem_limit_bytes=VMEM_LIMIT
        ),
    )(
        layer_input[0, 0], inner_acts[0, 0], out_grad[0, 0], step_sizes[0, 0], outer_weight, island_drift[0]
    )
    outer_delta = delta.reshape(512, 256).astype(F32)
    new_momentum = 0.9 * momentum + outer_delta
    new_outer = outer_weight - 0.7 * (outer_delta + 0.9 * new_momentum)
    return (in_grad[None, None], sel_grad[None, None], new_momentum, new_outer)


def solution(mesh):
    acts = P("island", "dp", "seq", None)
    rows = P(("seq", "dp"), None)
    return jax.shard_map(
        local,
        mesh=mesh,
        in_specs=(acts, acts, acts, acts, rows, P("island", ("seq", "dp"), None), rows),
        out_specs=(acts, acts, rows, rows),
        check_vma=False,
    )
```

time: 372 us -> 70.8 us (0.19)
  waiting for transfers between devices: 217 us -> 0 us
  matrix products: 67.3 us -> 0 us
  Pallas kernels: 0 us -> 63.2 us
  local copies, waits for them, and re-layouts: 44 us -> 4.87 us
  other arithmetic: 26.1 us -> 1.11 us
  between operations: 14 us -> 0.66 us
    reduce_scatter x1 -> x0, waiting for transfers between devices: 100 us -> none  [local(): lax.psum_scatter(jnp.einsum('td,tn->dn', columns, sel_grad, preferred_ele...]
    psum x1 -> x0, waiting for transfers between devices: 78.7 us -> none  [local(): outer_delta = lax.psum(pseudo, 'island') / lax.axis_size('island')]
    dot_general x12 -> x0, matrix products: 67.3 us -> none  [the longest x1 12.6 us: local(): jnp.einsum('sn,hnp->shp', input_map, adjoint_out, precision=lax.Precision...]
    pallas_call x0 -> x1, Pallas kernels: none -> 63.2 us  [local(): pl.pallas_call(kernel, out_shape=(jax.ShapeDtypeStruct((T, 8192), BF), ja...]
    all_gather x3 -> x0, waiting for transfers between devices: 38 us -> none  [the longest x1 34.8 us: local(): lax.all_gather(weight_rows, ('seq', 'dp'), axis=0, tiled=True)]
    unnamed x29 -> x10, local copies, waits for them, and re-layouts: 23.3 us -> 4.87 us
    add x1 -> x0, other arithmetic: 12.7 us -> none  [chain_states(): later[0][:, None, None] * earlier[1] + later[1]]
    dynamic_slice x2 -> x0, local copies, waits for them, and re-layouts: 11.6 us -> none  [one(): lax.dynamic_index_in_dim(a, source, 0, False)]
  transfers between devices with their start and end apart: 5 -> 0, of which waited for: 4 -> 0; matrix products, arithmetic and copies ran while one was open for 26% -> 0% of each run, Pallas kernels for 0% -> 0%
where the time goes in v1:
time: 70.8 us; the launch traced here: 69.8 us
  Pallas kernels  63.2 us (89%)
  local copies, waits for them, and re-layouts  4.87 us (7%)
  other arithmetic  1.11 us (2%)
    pallas_call x1, Pallas kernels, local(): pl.pallas_call(kernel, out_shape=(jax.ShapeDtypeStruct((T, 8192), BF), ja...  63.2 us
    unnamed x10, local copies, waits for them, and re-layouts  4.87 us

profile of v1, /device:TPU:6, one launch (start us, length us, event | category | flops | bytes accessed | tf_op | source)
XLA Modules:
  0.0 69.8 jit_solution(12952235561696611694)
XLA Ops:
  0.6 0.0 copy-start
  0.6 1.0 %copy-done = f32[512,256]{1,0:T(8,128)S(1)} copy-done((f32[512,256]{1,0:T(8,128)S(1)}, f32[512,256]{1,0:T(8,128)}, u32[]{:S(2)}) %copy-start) | copy-done | bytes 524312
  1.7 0.0 copy-start.1
  1.7 1.0 %copy-done.1 = f32[1,512,256]{2,1,0:T(8,128)S(1)} copy-done((f32[1,512,256]{2,1,0:T(8,128)S(1)}, f32[1,512,256]{2,1,0:T(8,128)}, u32[]{:S(2)}) %copy-start.1) | copy-done | bytes 524312
  2.7 0.0 copy-start.2
  2.7 0.8 %copy-done.2 = f32[1,1,128,128]{3,2,1,0:T(8,128)S(1)} copy-done((f32[1,1,128,128]{3,2,1,0:T(8,128)S(1)}, f32[1,1,128,128]{3,2,1,0:T(8,128)}, u32[]{:S(2)}) %copy-start.2) | copy-done | bytes 65560
  3.6 0.0 copy-start.3
  3.6 63.2 %shard_map.102 = (bf16[128,8192]{1,0:T(8,128)(2,1)S(1)}, bf16[128,256]{1,0:T(8,128)(2,1)S(1)}, bf16[4,4,32,256]{3,2,1,0:T(8,128)(2,1)S(1)}) custom-call(bf16[128,8192]{1,0:T(8,128)(2,1)} %bitcast.16, bf16[128,8192]{1,0:T(8,128)(2,1)} %bitcast.17, bf16[128,8192]{1,0:T(8,128)(2,1)} %bitcast.18, f32[128,128]{1,0:T(8,128)S(1)} %bitcast.14, ...), custom_call_target="tpu_custom_call" | custom-call | tf_op jit(solution)/shard_map/pallas_call | solution.py:393
  66.8 0.0 copy-done.3
  66.8 1.1 %fusion.1 = (f32[512,256]{1,0:T(8,128)}, f32[512,256]{1,0:T(8,128)}) fusion(f32[512,256]{1,0:T(8,128)S(1)} %copy-done, bf16[4,4,32,256]{3,2,1,0:T(8,128)(2,1)S(1)} %get-tuple-element.9, f32[512,256]{1,0:T(8,128)S(1)} %copy-done.3), kind=kLoop, calls=%fused_computation.3 | loop fusion | flops 917504 | bytes 2359296 | tf_op jit(solution)/shard_map/sub | solution.py:459
  67.9 1.3 %copy.13 = bf16[1,1,128,8192]{3,2,1,0:T(8,128)(2,1)} copy(bf16[1,1,128,8192]{3,2,1,0:T(8,128)(2,1)S(1)} %bitcast.12) | data formatting | bytes 4194304
  69.2 0.6 copy.14
Async XLA Ops:
  0.6 1.0 %copy-start = (f32[512,256]{1,0:T(8,128)S(1)}, f32[512,256]{1,0:T(8,128)}, u32[]{:S(2)}) copy-start(f32[512,256]{1,0:T(8,128)} %ow_hbm.1) | copy-start | bytes 1572868
  1.7 1.0 %copy-start.1 = (f32[1,512,256]{2,1,0:T(8,128)S(1)}, f32[1,512,256]{2,1,0:T(8,128)}, u32[]{:S(2)}) copy-start(f32[1,512,256]{2,1,0:T(8,128)} %param.12) | copy-start | bytes 1572868
  2.7 0.8 %copy-start.2 = (f32[1,1,128,128]{3,2,1,0:T(8,128)S(1)}, f32[1,1,128,128]{3,2,1,0:T(8,128)}, u32[]{:S(2)}) copy-start(f32[1,1,128,128]{3,2,1,0:T(8,128)} %param.10) | copy-start | bytes 196612
  3.6 63.2 %copy-start.3 = (f32[512,256]{1,0:T(8,128)S(1)}, f32[512,256]{1,0:T(8,128)}, u32[]{:S(2)}) copy-start(f32[512,256]{1,0:T(8,128)} %param.13) | copy-start | bytes 1572868

commit v2 on v1

--- a/solution.py
+++ b/solution.py
@@ -15,7 +15,9 @@
 T = 128
 NZ = 8
 NQ = 4
-VMEM_LIMIT = 50 * 1024 * 1024
+EVENTS = 14
+VMEM_LIMIT = 60 * 1024 * 1024
+FINISH_LIMIT = 62 * 1024 * 1024
 
 
 def dot(a, b, ca=1, cb=0):
@@ -35,7 +37,7 @@
     lq, lt, mixacc, ew, pw, ewx, gw, e_all, ig, mb, mt2, m2,
     psel, prem, sel, sall, gf, gs, r2, t2, t2b, r3, dl,
     loc, ring_s, ring_r, pair_s, pair_r, xr_s, xr_r, dr_s, dr_r,
-    s_s, s_r, p_s, p_r, z_s, z_r, a_s, a_r, b_s, b_r, outs,
+    s_s, s_r, p_s, p_r, z_s, z_r, a_s, a_r, outs,
 ):
     s = lax.axis_index("seq")
     z = lax.axis_index("dp")
@@ -78,30 +80,30 @@
     lax.fori_loop(0, 32, load_x, 0)
 
     barrier = pltpu.get_barrier_semaphore()
-    peers = [partner] + [along(k) for k in range(1, 8)] + [first(k) for k in range(1, 4)] + [second(k) for k in range(1, 4)]
+    peers = [partner] + [along(k) for k in range(1, 8)]
+    peers += [{"seq": s, "dp": z, "island": (isl + k) % 16} for k in range(1, 16)]
     for d in peers:
         pl.semaphore_signal(barrier, inc=1, device_id=d, device_id_type=MESH)
 
     c_ow.wait()
     c_dr.wait()
-    wg[z] = (ow[...] + dr[...]).astype(BF)
+    wg[z] = (ow[...] + dr[...]).astype(BF).reshape(4, 128, 256)
     for q in range(4):
         ds16[q] = dr[pl.ds(q * 128, 128), :].astype(BF)
 
     pl.semaphore_wait(barrier, len(peers))
 
-    def right(j, zb, half):
-        at = wg.at[zb, pl.ds(pl.multiple_of(half * 256, 256), 256)]
+    def right(j, zb, q):
+        at = wg.at[zb, q]
         return remote(at, at, ring_s.at[0, j], ring_r.at[0, j], along(1))
 
-    def left(j, zb, half):
-        at = wg.at[zb, pl.ds(pl.multiple_of(half * 256, 256), 256)]
+    def left(j, zb, q):
+        at = wg.at[zb, q]
         return remote(at, at, ring_s.at[1, j], ring_r.at[1, j], along(7))
 
-    right(0, z, 0).start()
-    left(0, z, 1).start()
-    right(1, z, 1).start()
-    left(1, z, 0).start()
+    for j in range(4):
+        right(j, z, j).start()
+        left(j, z, 3 - j).start()
 
     def send_x(c, carry):
         col = pl.multiple_of((1 - s) * 4096 + c * 128, 128)
@@ -189,47 +191,36 @@
                 e_all[g * 8 + c] = e.astype(BF)
         mixacc[...] = mix
 
-    def partial_sel(zb, half):
-        a = jnp.concatenate([xs[2 * half, zb], xs[2 * half + 1, zb]], axis=1)
-        return dot(a, wg[zb, pl.ds(pl.multiple_of(half * 256, 256), 256), :])
-
-    psel[...] = partial_sel(z, 0) + partial_sel(z, 1)
-    group(14)
-    group(15)
-
-    def event(j, carry):
-        k = j // 2 + 1
-        hr = j % 2
-        hl = 1 - hr
+    def two_parts(za, qa, zb, qb):
+        a = jnp.concatenate([xs[qa, za], xs[qb, zb]], axis=1)
+        b = jnp.concatenate([wg[za, qa], wg[zb, qb]], axis=0)
+        return dot(a, b)
+
+    def event(j, forward):
+        k = j // 4 + 1
+        qr = j % 4
+        ql = 3 - qr
         zr = (z - k + 8) % 8
         zl = (z + k) % 8
-        right(j, zr, hr).wait_recv()
-
-        @pl.when(j < 5)
-        def _():
-            right(j + 2, zr, hr).start()
-
-        left(j, zl, hl).wait_recv()
-
-        @pl.when(j < 5)
-        def _():
-            left(j + 2, zl, hl).start()
-
-        psel[...] += partial_sel(zr, hr) + partial_sel(zl, hl)
-
-        @pl.when(j < 6)
-        def _():
-            group(2 * j)
-            group(2 * j + 1)
-
-        return carry
-
-    group(12)
-    group(13)
-    lax.fori_loop(0, 7, event, 0)
-
-    c_psel = remote(psel, prem, pair_s.at[2], pair_r.at[2], partner)
-    c_psel.start()
+        right(j, zr, qr).wait_recv()
+        if forward:
+            right(j + 4, zr, qr).start()
+        left(j, zl, ql).wait_recv()
+        if forward:
+            left(j + 4, zl, ql).start()
+        psel[...] += two_parts(zr, qr, zl, ql)
+
+    psel[...] = two_parts(z, 0, z, 1) + two_parts(z, 2, z, 3)
+    group(0)
+    group(1)
+
+    def busy(j, carry):
+        event(j, True)
+        group(2 * j + 2)
+        group(2 * j + 3)
+        return carry
+
+    lax.fori_loop(0, 7, busy, 0)
 
     c_mb0 = remote(mb.at[pl.ds(0, 2)], mb.at[pl.ds(0, 2)], pair_s.at[3], pair_r.at[3], partner)
     c_mb1 = remote(mb.at[2], mb.at[2], pair_s.at[4], pair_r.at[4], partner)
@@ -240,12 +231,21 @@
         mb[0] = mixacc[...]
         mb[1] = dot(pw[...], gw[...], 1, 1)
         c_mb0.start()
-        c_mb1.wait_recv()
 
     @pl.when(s == 1)
     def _():
         mb[2] = mixacc[...]
         c_mb1.start()
+
+    for j in range(7, 10):
+        event(j, True)
+
+    @pl.when(s == 0)
+    def _():
+        c_mb1.wait_recv()
+
+    @pl.when(s == 1)
+    def _():
         c_mb0.wait_recv()
 
     mt = jnp.concatenate(
@@ -264,15 +264,23 @@
         return carry
 
     lax.fori_loop(0, 8, turn_own, 0)
-    for k in range(1, 4):
+
+    for j in range(10, 14):
+        event(j, False)
+        k = j - 9
+        if k == 4:
+            break
         remote(xs.at[(p1 + k) % 4], xr.at[k - 1], xr_s.at[k - 1], xr_r.at[k - 1], first(k)).wait_recv()
 
-        def turn(zb, carry):
+        def turn(zb, carry, k=k):
             xt[zb, :, k * 256 : (k + 1) * 256] = xr[k - 1, zb].T
             return carry
 
         lax.fori_loop(0, 8, turn, 0)
         remote(ds16.at[(p1 + k) % 4], dr16.at[k - 1], dr_s.at[k - 1], dr_r.at[k - 1], first(k)).wait_recv()
+
+    c_psel = remote(psel, prem, pair_s.at[2], pair_r.at[2], partner)
+    c_psel.start()
 
     c_psel.wait_recv()
     sel[...] = ((psel[...] + prem[...]) * (1.0 / math.sqrt(8192.0))).astype(BF)
@@ -302,7 +310,7 @@
 
         lax.fori_loop(start, stop, one, 0)
 
-    grads(0, 24)
+    grads(0, 26)
 
     for k in range(1, 4):
         remote(sall.at[0], sall.at[k], s_s.at[k - 1], s_r.at[k - 1], first(k)).wait_recv()
@@ -322,7 +330,7 @@
         gs[q] = gf[:, q * 32 : (q + 1) * 32, :].astype(BF)
     for k in range(1, 4):
         remote(gs.at[(p2 + k) % 4], r2.at[k - 1], p_s.at[k - 1], p_r.at[k - 1], second(k)).start()
-    grads(24, 40)
+    grads(26, 48)
     total = gf[:, pl.ds(pl.multiple_of(p2 * 32, 32), 32), :]
     for k in range(1, 4):
         remote(gs.at[(p2 + k) % 4], r2.at[k - 1], p_s.at[k - 1], p_r.at[k - 1], second(k)).wait_recv()
@@ -331,26 +339,36 @@
     t2b[...] = total.astype(BF)
     for k in range(1, 8):
         remote(t2b.at[(z + k) % 8], r3.at[k - 1], z_s.at[k - 1], z_r.at[k - 1], along(k)).start()
-    grads(40, 52)
+    grads(48, 64)
+    c_ig = pltpu.make_async_copy(ig, ig_hbm, outs.at[1])
+    c_ig.start()
     part = t2[z]
     for k in range(1, 8):
         remote(t2b.at[(z + k) % 8], r3.at[k - 1], z_s.at[k - 1], z_r.at[k - 1], along(k)).wait_recv()
         part = part + r3[k - 1].astype(F32)
-    dl[p1, p2] = (part * (1.0 / 16.0)).astype(BF)
-    for k in range(1, 4):
-        remote(dl.at[p1, p2], dl.at[p1, p2], a_s.at[k - 1], a_r.at[k - 1], second(k)).start()
-    grads(52, 58)
-    for k in range(1, 4):
-        at = dl.at[p1, (p2 + 4 - k) % 4]
-        remote(at, at, a_s.at[k - 1], a_r.at[k - 1], second(k)).wait_recv()
-    for k in range(1, 4):
-        remote(dl.at[p1], dl.at[p1], b_s.at[k - 1], b_r.at[k - 1], first(k)).start()
-    grads(58, 64)
-    c_ig = pltpu.make_async_copy(ig, ig_hbm, outs.at[1])
-    c_ig.start()
-    for k in range(1, 4):
-        at = dl.at[(p1 + 4 - k) % 4]
-        remote(at, at, b_s.at[k - 1], b_r.at[k - 1], first(k)).wait_recv()
+    mine_at = p1 * 4 + p2
+    dl[mine_at] = (part * (1.0 / 16.0)).astype(BF)
+
+    def plane(k):
+        return remote(
+            dl.at[mine_at], dl.at[mine_at], a_s.at[k - 1], a_r.at[k - 1], {"seq": s, "dp": z, "island": (isl + k) % 16}
+        )
+
+    def share(k, carry):
+        plane(k).start()
+        return carry
+
+    lax.fori_loop(1, 16, share, 0)
+
+    def arrived(k, carry):
+        other = (isl + 16 - k) % 16
+        oy = other // 4
+        ox = other % 4
+        at = dl.at[(ox + s * (oy - ox)) * 4 + oy + s * (ox - oy)]
+        remote(at, at, a_s.at[k - 1], a_r.at[k - 1], partner).wait_recv()
+        return carry
+
+    lax.fori_loop(1, 16, arrived, 0)
     c_delta = pltpu.make_async_copy(dl, delta_hbm, outs.at[2])
     c_delta.start()
 
@@ -359,7 +377,7 @@
         left(j, z, 0).wait_send()
         return carry
 
-    lax.fori_loop(0, 7, drain, 0)
+    lax.fori_loop(0, EVENTS, drain, 0)
     remote(own_x, other_x, pair_s.at[0], pair_r.at[0], partner).wait_send()
     c_psel.wait_send()
 
@@ -377,13 +395,49 @@
         remote(ds16.at[0], dr16.at[k - 1], dr_s.at[k - 1], dr_r.at[k - 1], first(k)).wait_send()
         remote(sall.at[0], sall.at[k], s_s.at[k - 1], s_r.at[k - 1], first(k)).wait_send()
         remote(gs.at[0], r2.at[k - 1], p_s.at[k - 1], p_r.at[k - 1], second(k)).wait_send()
-        remote(dl.at[p1, p2], dl.at[p1, p2], a_s.at[k - 1], a_r.at[k - 1], second(k)).wait_send()
-        remote(dl.at[p1], dl.at[p1], b_s.at[k - 1], b_r.at[k - 1], first(k)).wait_send()
     for k in range(1, 8):
         remote(t2b.at[0], r3.at[k - 1], z_s.at[k - 1], z_r.at[k - 1], along(k)).wait_send()
+
+    def left_here(k, carry):
+        plane(k).wait_send()
+        return carry
+
+    lax.fori_loop(1, 16, left_here, 0)
     c_sg.wait()
     c_ig.wait()
     c_delta.wait()
+
+
+def finish(ig, sg, dl, mo, ow, ig_out, sg_out, mo_out, ow_out, igv, sgv, dlv, mov, owv, nmv, nov, ins, outs):
+    loads = [
+        pltpu.make_async_copy(dl, dlv, ins.at[0]),
+        pltpu.make_async_copy(mo, mov, ins.at[1]),
+        pltpu.make_async_copy(ow, owv, ins.at[2]),
+        pltpu.make_async_copy(sg, sgv, ins.at[3]),
+    ]
+    parts = [pl.ds(2048 * c, 2048) for c in range(4)]
+    moves = [pltpu.make_async_copy(ig.at[:, p], igv.at[:, p], ins.at[4 + c]) for c, p in enumerate(parts)]
+    for c in loads + moves:
+        c.start()
+    ends = []
+    for c, p in enumerate(parts):
+        moves[c].wait()
+        ends.append(pltpu.make_async_copy(igv.at[:, p], ig_out.at[:, p], outs.at[4 + c]))
+        ends[c].start()
+    for c in loads:
+        c.wait()
+    c_sg = pltpu.make_async_copy(sgv, sg_out, outs.at[1])
+    c_sg.start()
+    delta = dlv[...].reshape(512, 256).astype(F32)
+    momentum = 0.9 * mov[...] + delta
+    nmv[...] = momentum
+    c_mo = pltpu.make_async_copy(nmv, mo_out, outs.at[2])
+    c_mo.start()
+    nov[...] = owv[...] - 0.7 * (delta + 0.9 * momentum)
+    c_ow = pltpu.make_async_copy(nov, ow_out, outs.at[3])
+    c_ow.start()
+    for c in ends + [c_sg, c_mo, c_ow]:
+        c.wait()
 
 
 def local(layer_input, inner_acts, out_grad, step_sizes, outer_weight, island_drift, momentum):
@@ -395,9 +449,9 @@
         out_shape=(
             jax.ShapeDtypeStruct((T, 8192), BF),
             jax.ShapeDtypeStruct((T, 256), BF),
-            jax.ShapeDtypeStruct((4, 4, 32, 256), BF),
+            jax.ShapeDtypeStruct((16, 32, 256), BF),
         ),
-        in_specs=[anyspec] * 6,
+        in_specs=[pl.BlockSpec(memory_space=pltpu.HBM)] * 6,
         out_specs=(anyspec, anyspec, anyspec),
         scratch_shapes=[
             vm((512, 256), F32),
@@ -405,7 +459,7 @@
             vm((T, HEADS), F32),
             vm((T, 8192), BF),
             vm((T, 8192), BF),
-            vm((8, 512, 256), BF),
+            vm((8, 4, 128, 256), BF),
             vm((4, 8, 256, 128), BF),
             vm((3, 8, 256, 128), BF),
             vm((8, 128, 1024), BF),
@@ -433,10 +487,10 @@
             vm((8, 32, 256), F32),
             vm((8, 32, 256), BF),
             vm((7, 32, 256), BF),
-            vm((4, 4, 32, 256), BF),
+            vm((16, 32, 256), BF),
             dma((6,)),
-            dma((2, 7)),
-            dma((2, 7)),
+            dma((2, EVENTS)),
+            dma((2, EVENTS)),
             dma((5,)),
             dma((5,)),
             dma((3,)), dma((3,)),
@@ -444,8 +498,7 @@
             dma((3,)), dma((3,)),
             dma((3,)), dma((3,)),
             dma((7,)), dma((7,)),
-            dma((3,)), dma((3,)),
-            dma((3,)), dma((3,)),
+            dma((15,)), dma((15,)),
             dma((3,)),
         ],
         compiler_params=pltpu.CompilerParams(
@@ -454,9 +507,23 @@
     )(
         layer_input[0, 0], inner_acts[0, 0], out_grad[0, 0], step_sizes[0, 0], outer_weight, island_drift[0]
     )
-    outer_delta = delta.reshape(512, 256).astype(F32)
-    new_momentum = 0.9 * momentum + outer_delta
-    new_outer = outer_weight - 0.7 * (outer_delta + 0.9 * new_momentum)
+    in_grad, sel_grad, new_momentum, new_outer = pl.pallas_call(
+        finish,
+        out_shape=(
+            jax.ShapeDtypeStruct((T, 8192), BF),
+            jax.ShapeDtypeStruct((T, 256), BF),
+            jax.ShapeDtypeStruct((512, 256), F32),
+            jax.ShapeDtypeStruct((512, 256), F32),
+        ),
+        in_specs=[anyspec] * 5,
+        out_specs=(pl.BlockSpec(memory_space=pltpu.HBM),) * 4,
+        scratch_shapes=[
+            vm((T, 8192), BF), vm((T, 256), BF), vm((16, 32, 256), BF),
+            vm((512, 256), F32), vm((512, 256), F32), vm((512, 256), F32), vm((512, 256), F32),
+            dma((8,)), dma((8,)),
+        ],
+        compiler_params=pltpu.CompilerParams(vmem_limit_bytes=FINISH_LIMIT),
+    )(in_grad, sel_grad, delta, momentum, outer_weight)
     return (in_grad[None, None], sel_grad[None, None], new_momentum, new_outer)
 
 

time: 70.8 us -> 63.5 us (0.90); the launches traced: 69.8 us -> 63.4 us
  local copies, waits for them, and re-layouts: 4.87 us -> 0 us
  other arithmetic: 1.11 us -> 0 us
    unnamed x10 -> x0, local copies, waits for them, and re-layouts: 4.87 us -> none
    pallas_call x1, Pallas kernels: 63.2 us -> 59.5 us  [local(): pl.pallas_call(kernel, out_shape=(jax.ShapeDtypeStruct((T, 8192), BF), ja...]
    pallas_call x0 -> x1, Pallas kernels: none -> 3.28 us  [local(): pl.pallas_call(finish, out_shape=(jax.ShapeDtypeStruct((T, 8192), BF), ja...]
    sub x1 -> x0, other arithmetic: 1.11 us -> none  [local(): new_outer = outer_weight - 0.7 * (outer_delta + 0.9 * new_momentum)]
where the time goes in v2:
time: 63.5 us; the launch traced here: 63.4 us
  Pallas kernels  62.7 us (99%)
  between operations  0.64 us (1%)
    pallas_call x1, Pallas kernels, local(): pl.pallas_call(kernel, out_shape=(jax.ShapeDtypeStruct((T, 8192), BF), ja...  59.5 us
    pallas_call x1, Pallas kernels, local(): pl.pallas_call(finish, out_shape=(jax.ShapeDtypeStruct((T, 8192), BF), ja...  3.28 us

profile of v2, /device:TPU:6, one launch (start us, length us, event | category | flops | bytes accessed | tf_op | source)
XLA Modules:
  0.0 63.4 jit_solution(8484211049222490631)
XLA Ops:
  0.6 59.5 %shard_map.102 = (bf16[128,8192]{1,0:T(8,128)(2,1)}, bf16[128,256]{1,0:T(8,128)(2,1)}, bf16[16,32,256]{2,1,0:T(8,128)(2,1)}) custom-call(bf16[128,8192]{1,0:T(8,128)(2,1)} %bitcast.7, bf16[128,8192]{1,0:T(8,128)(2,1)} %bitcast.8, bf16[128,8192]{1,0:T(8,128)(2,1)} %bitcast.9, f32[128,128]{1,0:T(8,128)} %bitcast.11, f32[512,256]{1,0:T(8,128)} %ow.1, ...), custom_call_target="tpu_custom_call" | custom-call | tf_op jit(solution)/shard_map/pallas_call | solution.py:447
  60.1 3.3 %shard_map.103 = (bf16[128,8192]{1,0:T(8,128)(2,1)}, bf16[128,256]{1,0:T(8,128)(2,1)}, f32[512,256]{1,0:T(8,128)}, f32[512,256]{1,0:T(8,128)}) custom-call(bf16[128,8192]{1,0:T(8,128)(2,1)} %get-tuple-element.11.ig, bf16[128,256]{1,0:T(8,128)(2,1)} %get-tuple-element.12.sg, bf16[16,32,256]{2,1,0:T(8,128)(2,1)} %get-tuple-element.13.dl, f32[512,256]{1,0:T(8,128)} %mo.1, ...), custom_call_target="tpu_custom_call" | custom-call | tf_op jit(solution)/shard_map/pallas_call | solution.py:510

commit v3 on v2

--- a/solution.py
+++ b/solution.py
@@ -62,6 +62,11 @@
 
     partner = {"seq": 1 - s, "dp": z, "island": isl}
 
+    barrier = pltpu.get_barrier_semaphore()
+    peers = [partner, along(1), along(7)] + [d(k) for d in (first, second) for k in (1, 2, 3)]
+    for d in peers:
+        pl.semaphore_signal(barrier, inc=1, device_id=d, device_id_type=MESH)
+
     c_ow = pltpu.make_async_copy(ow_hbm, ow, loc.at[0])
     c_dr = pltpu.make_async_copy(dr_hbm, dr, loc.at[1])
     c_dt = pltpu.make_async_copy(dt_hbm, dt, loc.at[2])
@@ -70,28 +75,20 @@
     for c in (c_ow, c_dr, c_dt, c_dy, c_ia):
         c.start()
 
-    def load_x(c, carry):
-        col = pl.multiple_of(s * 4096 + c * 128, 128)
-        pltpu.make_async_copy(
-            x_hbm.at[:, pl.ds(col, 128)], xs.at[c % 4, c // 4, pl.ds(pl.multiple_of(s * T, T), T)], loc.at[5]
-        ).start()
-        return carry
-
-    lax.fori_loop(0, 32, load_x, 0)
-
-    barrier = pltpu.get_barrier_semaphore()
-    peers = [partner] + [along(k) for k in range(1, 8)]
-    peers += [{"seq": s, "dp": z, "island": (isl + k) % 16} for k in range(1, 16)]
-    for d in peers:
-        pl.semaphore_signal(barrier, inc=1, device_id=d, device_id_type=MESH)
+    mine = pl.ds(pl.multiple_of(s * T, T), T)
+    theirs = pl.ds(pl.multiple_of((1 - s) * T, T), T)
+    kept = pl.ds(pl.multiple_of(s * 4096, 128), 4096)
+    given = pl.ds(pl.multiple_of((1 - s) * 4096, 128), 4096)
+    c_x = pltpu.make_async_copy(x_hbm.at[:, kept], xs.at[mine], loc.at[5])
+    c_x.start()
 
     c_ow.wait()
     c_dr.wait()
     wg[z] = (ow[...] + dr[...]).astype(BF).reshape(4, 128, 256)
-    for q in range(4):
-        ds16[q] = dr[pl.ds(q * 128, 128), :].astype(BF)
-
     pl.semaphore_wait(barrier, len(peers))
+
+    c_xs = remote(x_hbm.at[:, given], xs.at[mine], pair_s.at[0], pair_r.at[0], partner)
+    c_xs.start()
 
     def right(j, zb, q):
         at = wg.at[zb, q]
@@ -105,15 +102,50 @@
         right(j, z, j).start()
         left(j, z, 3 - j).start()
 
-    def send_x(c, carry):
-        col = pl.multiple_of((1 - s) * 4096 + c * 128, 128)
-        remote(
-            x_hbm.at[:, pl.ds(col, 128)], xs.at[c % 4, c // 4, pl.ds(pl.multiple_of(s * T, T), T)],
-            pair_s.at[0], pair_r.at[0], partner,
-        ).start()
-        return carry
-
-    lax.fori_loop(0, 32, send_x, 0)
+    for q in range(4):
+        ds16[q] = dr[pl.ds(q * 128, 128), :].astype(BF)
+
+    def columns(zb, q):
+        return pl.ds(pl.multiple_of(zb * 512 + q * 128, 128), 128)
+
+    def send_xr(k, zb):
+        return remote(
+            xs.at[:, columns(zb, (p1 + k) % 4)], xr.at[k - 1, zb], xr_s.at[k - 1], xr_r.at[k - 1], first(k)
+        )
+
+    def all_xr(k):
+        return remote(xr.at[k - 1], xr.at[k - 1], xr_s.at[k - 1], xr_r.at[k - 1], first(k))
+
+    def send_dr(k):
+        return remote(ds16.at[(p1 + k) % 4], dr16.at[k - 1], dr_s.at[k - 1], dr_r.at[k - 1], first(k))
+
+    def spread(k):
+        def one(zb, carry):
+            send_xr(k, zb).start()
+            return carry
+
+        lax.fori_loop(0, 8, one, 0)
+        send_dr(k).start()
+
+    def event(j, forward):
+        k = j // 4 + 1
+        qr = j % 4
+        ql = 3 - qr
+        zr = (z - k + 8) % 8
+        zl = (z + k) % 8
+        right(j, zr, qr).wait_recv()
+        if forward is not None:
+
+            @pl.when(forward)
+            def _():
+                right(j + 4, zr, qr).start()
+
+        left(j, zl, ql).wait_recv()
+        if forward is not None:
+
+            @pl.when(forward)
+            def _():
+                left(j + 4, zl, ql).start()
 
     c_dt.wait()
     rows = lax.broadcasted_iota(jnp.int32, (T, T), 0)
@@ -132,9 +164,6 @@
     hi = factor.astype(BF)
     ew[:, 0:T] = hi
     ew[:, T : 2 * T] = (factor - hi.astype(F32)).astype(BF)
-    c_ia.wait()
-    c_dy.wait()
-
     def widen(c, carry):
         wide = 512
         kk = lax.broadcasted_iota(jnp.int32, (2 * T, wide), 0)
@@ -154,21 +183,29 @@
 
         return carry
 
-    lax.fori_loop(0, 16, widen, 0)
-
     c_gw = remote(gw, gw, pair_s.at[1], pair_r.at[1], partner)
+    always = s >= 0
+    c_x.wait()
+    remote(xs.at[theirs], xs.at[theirs], pair_s.at[0], pair_r.at[0], partner).wait_recv()
+    spread(1)
+    spread(2)
+    spread(3)
+    event(0, always)
+    c_ia.wait()
+    c_dy.wait()
+    lax.fori_loop(0, 5, widen, 0)
+    event(1, always)
+    lax.fori_loop(5, 11, widen, 0)
+    event(2, always)
+    lax.fori_loop(11, 16, widen, 0)
 
     @pl.when(s == 1)
     def _():
         c_gw.start()
 
-    own_x = xs.at[:, :, pl.ds(pl.multiple_of(s * T, T), T)]
-    pltpu.make_async_copy(own_x, own_x, loc.at[5]).wait()
-    other_x = xs.at[:, :, pl.ds(pl.multiple_of((1 - s) * T, T), T)]
-    remote(own_x, other_x, pair_s.at[0], pair_r.at[0], partner).wait_recv()
-    for k in range(1, 4):
-        remote(xs.at[(p1 + k) % 4], xr.at[k - 1], xr_s.at[k - 1], xr_r.at[k - 1], first(k)).start()
-        remote(ds16.at[(p1 + k) % 4], dr16.at[k - 1], dr_s.at[k - 1], dr_r.at[k - 1], first(k)).start()
+    event(3, always)
+    event(4, always)
+    event(5, always)
 
     mixacc[...] = jnp.zeros((T, T), F32)
     low = lax.broadcasted_iota(jnp.int32, (T, T), 1) < 64
@@ -192,35 +229,33 @@
         mixacc[...] = mix
 
     def two_parts(za, qa, zb, qb):
-        a = jnp.concatenate([xs[qa, za], xs[qb, zb]], axis=1)
+        a = jnp.concatenate([xs[:, columns(za, qa)], xs[:, columns(zb, qb)]], axis=1)
         b = jnp.concatenate([wg[za, qa], wg[zb, qb]], axis=0)
         return dot(a, b)
 
-    def event(j, forward):
+    def add(both, start):
+        for c in range(2):
+            half = both[:, c * T : (c + 1) * T]
+            psel[c] = half if start else psel[c] + half
+
+    def gain(j, carry):
         k = j // 4 + 1
-        qr = j % 4
-        ql = 3 - qr
-        zr = (z - k + 8) % 8
-        zl = (z + k) % 8
-        right(j, zr, qr).wait_recv()
-        if forward:
-            right(j + 4, zr, qr).start()
-        left(j, zl, ql).wait_recv()
-        if forward:
-            left(j + 4, zl, ql).start()
-        psel[...] += two_parts(zr, qr, zl, ql)
-
-    psel[...] = two_parts(z, 0, z, 1) + two_parts(z, 2, z, 3)
-    group(0)
-    group(1)
+        add(two_parts((z - k + 8) % 8, j % 4, (z + k) % 8, 3 - j % 4), False)
+        return carry
+
+    def group_loop(g, carry):
+        group(g)
+        return carry
 
     def busy(j, carry):
-        event(j, True)
-        group(2 * j + 2)
-        group(2 * j + 3)
-        return carry
-
-    lax.fori_loop(0, 7, busy, 0)
+        event(j, j < 10)
+        lax.fori_loop(3 * j - 18, 3 * j - 15, group_loop, 0)
+        return gain(j - 6, carry)
+
+    add(two_parts(z, 0, z, 1) + two_parts(z, 2, z, 3), True)
+    lax.fori_loop(6, 11, busy, 0)
+    event(11, None)
+    group(15)
 
     c_mb0 = remote(mb.at[pl.ds(0, 2)], mb.at[pl.ds(0, 2)], pair_s.at[3], pair_r.at[3], partner)
     c_mb1 = remote(mb.at[2], mb.at[2], pair_s.at[4], pair_r.at[4], partner)
@@ -237,9 +272,15 @@
         mb[2] = mixacc[...]
         c_mb1.start()
 
-    for j in range(7, 10):
-        event(j, True)
-
+    lax.fori_loop(5, 12, gain, 0)
+    event(12, None)
+    gain(12, 0)
+
+    def turn_own(zb, carry):
+        xt[pl.ds(pl.multiple_of(zb * 128, 128), 128), 0:256] = xs[:, columns(zb, p1)].T
+        return carry
+
+    lax.fori_loop(0, 8, turn_own, 0)
     @pl.when(s == 0)
     def _():
         c_mb1.wait_recv()
@@ -259,106 +300,141 @@
     m2[0] = mh
     m2[1] = (m - mh.astype(F32)).astype(BF)
 
-    def turn_own(zb, carry):
-        xt[zb, :, 0:256] = xs[p1, zb].T
-        return carry
-
-    lax.fori_loop(0, 8, turn_own, 0)
-
-    for j in range(10, 14):
-        event(j, False)
-        k = j - 9
-        if k == 4:
-            break
-        remote(xs.at[(p1 + k) % 4], xr.at[k - 1], xr_s.at[k - 1], xr_r.at[k - 1], first(k)).wait_recv()
-
-        def turn(zb, carry, k=k):
-            xt[zb, :, k * 256 : (k + 1) * 256] = xr[k - 1, zb].T
-            return carry
-
-        lax.fori_loop(0, 8, turn, 0)
-        remote(ds16.at[(p1 + k) % 4], dr16.at[k - 1], dr_s.at[k - 1], dr_r.at[k - 1], first(k)).wait_recv()
-
+    event(13, None)
+    gain(13, 0)
     c_psel = remote(psel, prem, pair_s.at[2], pair_r.at[2], partner)
     c_psel.start()
 
+    inv_root = 1.0 / math.sqrt(8192.0)
+
+    scale = 0.5 * inv_root
+
+    place = {1: 1, 3: 2, 2: 3}
+
+    def send_s(k):
+        return remote(sall.at[0], sall.at[place[k]], s_s.at[k - 1], s_r.at[k - 1], first(k))
+
     c_psel.wait_recv()
-    sel[...] = ((psel[...] + prem[...]) * (1.0 / math.sqrt(8192.0))).astype(BF)
-    bmap = sel[:, 0:T]
-    cmap = sel[:, T : 2 * T]
+    bmap = ((psel[0] + prem[0]) * inv_root).astype(BF)
+    cmap = ((psel[1] + prem[1]) * inv_root).astype(BF)
     d_in = dot(mt2[0], cmap) + dot(mt2[1], cmap)
     d_out = dot(m2[0], bmap) + dot(m2[1], bmap)
     sall[0] = jnp.concatenate([d_in, d_out], axis=1).astype(BF)
-    for k in range(1, 4):
-        remote(sall.at[0], sall.at[k], s_s.at[k - 1], s_r.at[k - 1], first(k)).start()
-    c_sg = pltpu.make_async_copy(sall.at[0, pl.ds(pl.multiple_of(s * T, T), T)], sg_hbm, outs.at[0])
+    for k in (2, 1, 3):
+        send_s(k).start()
+    c_sg = pltpu.make_async_copy(sall.at[0, mine], sg_hbm, outs.at[0])
     c_sg.start()
-
-    mine = pl.ds(pl.multiple_of(s * T, T), T)
+    sel[:, 0:T] = bmap
+    sel[:, T : 2 * T] = cmap
+
     inter = dot(sel[mine, 0:T], sel[mine, T : 2 * T], 1, 1).astype(BF)
     across = (dot(sel[0:T, 0:T], sel[T : 2 * T, T : 2 * T], 1, 1) * (1 - s).astype(F32)).astype(BF)
 
     def grads(start, stop):
         def one(j, carry):
-            off = pl.ds(pl.multiple_of(j * 128, 128), 128)
-            dp = dy[:, off]
-            lhs = jnp.concatenate([e_all[2 * j] * inter, e_all[2 * j + 1] * inter], axis=1)
-            rhs = jnp.concatenate([jnp.where(low, dp, none), jnp.where(low, none, dp)], axis=0)
-            out = dot(lhs, rhs) + ewx[:, off].astype(F32) * dot(across, gw[:, off])
-            ig[:, off] = out.astype(BF)
+            for u in range(4):
+                pair = 4 * j + u
+                off = pl.ds(pl.multiple_of(pair * 128, 128), 128)
+                dp = dy[:, off]
+                lhs = jnp.concatenate([e_all[2 * pair] * inter, e_all[2 * pair + 1] * inter], axis=1)
+                rhs = jnp.concatenate([jnp.where(low, dp, none), jnp.where(low, none, dp)], axis=0)
+                out = dot(lhs, rhs) + ewx[:, off].astype(F32) * dot(across, gw[:, off])
+                ig[:, off] = out.astype(BF)
             return carry
 
-        lax.fori_loop(start, stop, one, 0)
-
-    grads(0, 26)
-
+        lax.fori_loop(start // 4, stop // 4, one, 0)
+
+    def ig_out(c):
+        part = pl.ds(c * 2048, 2048)
+        return pltpu.make_async_copy(ig.at[:, part], ig_hbm.at[:, part], outs.at[1 + c])
+
+    def blocks(half):
+        return pl.ds(pl.multiple_of(half * 4, 4), 4), pl.ds(pl.multiple_of(half * 512, 512), 512)
+
+    def own_weight(half, carry):
+        four, rows_of = blocks(half)
+        gf[four] = dot(xt[rows_of, 0:256], sall[0]).reshape(4, 128, 256)
+        return carry
+
+    lax.fori_loop(0, 2, own_weight, 0)
     for k in range(1, 4):
-        remote(sall.at[0], sall.at[k], s_s.at[k - 1], s_r.at[k - 1], first(k)).wait_recv()
-
-    scale = 0.5 / math.sqrt(8192.0)
-
-    def weight(zb, carry):
-        gf[zb] = dot(xt[zb], sall[...].reshape(1024, 256)) * scale
-        return carry
-
-    lax.fori_loop(0, 8, weight, 0)
+        all_xr(k).wait_recv()
+
+        def turn(zb, carry, k=k):
+            at = place[k] * 256
+            xt[pl.ds(pl.multiple_of(zb * 128, 128), 128), at : at + 256] = xr[k - 1, zb].T
+            return carry
+
+        lax.fori_loop(0, 8, turn, 0)
+        send_dr(k).wait_recv()
     drift = dr[pl.ds(pl.multiple_of(p1 * 128, 128), 128), :]
     for k in range(3):
         drift = drift + dr16[k].astype(F32)
-    gf[z] = gf[z] - drift
-    for q in range(4):
-        gs[q] = gf[:, q * 32 : (q + 1) * 32, :].astype(BF)
-    for k in range(1, 4):
-        remote(gs.at[(p2 + k) % 4], r2.at[k - 1], p_s.at[k - 1], p_r.at[k - 1], second(k)).start()
-    grads(26, 48)
+    gf[z] = gf[z] - drift * (1.0 / scale)
+    grads(0, 16)
+    ig_out(0).start()
+
+    def send_p(k):
+        return remote(gs.at[(p2 + k) % 4], r2.at[k - 1], p_s.at[k - 1], p_r.at[k - 1], second(k))
+
+    send_s(1).wait_recv()
+    send_s(3).wait_recv()
+
+    def near_weight(half, carry):
+        four, rows_of = blocks(half)
+        gf[four] += dot(xt[rows_of, 256:768], sall[1:3].reshape(512, 256)).reshape(4, 128, 256)
+        return carry
+
+    lax.fori_loop(0, 2, near_weight, 0)
+    send_s(2).wait_recv()
+
+    def far_weight(half, carry):
+        four, rows_of = blocks(half)
+        g = (gf[four] + dot(xt[rows_of, 768:1024], sall[3]).reshape(4, 128, 256)) * scale
+        gf[four] = g
+        for q in range(4):
+            gs[q, four] = g[:, q * 32 : (q + 1) * 32].astype(BF)
+        return carry
+
+    lax.fori_loop(0, 2, far_weight, 0)
+    for k in (2, 1, 3):
+        send_p(k).start()
+    grads(16, 32)
+    ig_out(1).start()
+
+    def send_z(k):
+        return remote(t2b.at[(z + k) % 8], r3.at[k - 1], z_s.at[k - 1], z_r.at[k - 1], along(k))
+
     total = gf[:, pl.ds(pl.multiple_of(p2 * 32, 32), 32), :]
-    for k in range(1, 4):
-        remote(gs.at[(p2 + k) % 4], r2.at[k - 1], p_s.at[k - 1], p_r.at[k - 1], second(k)).wait_recv()
+    for k in (1, 3, 2):
+        send_p(k).wait_recv()
         total = total + r2[k - 1].astype(F32)
     t2[...] = total
     t2b[...] = total.astype(BF)
-    for k in range(1, 8):
-        remote(t2b.at[(z + k) % 8], r3.at[k - 1], z_s.at[k - 1], z_r.at[k - 1], along(k)).start()
-    grads(48, 64)
-    c_ig = pltpu.make_async_copy(ig, ig_hbm, outs.at[1])
-    c_ig.start()
+    for k in (4, 3, 5, 2, 6, 1, 7):
+        send_z(k).start()
+    grads(32, 48)
+    ig_out(2).start()
+    mine_at = p1 * 4 + p2
+
+    def plane(k):
+        at = dl.at[mine_at]
+        device = {"seq": s, "dp": z, "island": (isl + k) % 16}
+        return remote(at, at, a_s.at[k - 1], a_r.at[k - 1], device)
+
     part = t2[z]
     for k in range(1, 8):
-        remote(t2b.at[(z + k) % 8], r3.at[k - 1], z_s.at[k - 1], z_r.at[k - 1], along(k)).wait_recv()
+        send_z(k).wait_recv()
         part = part + r3[k - 1].astype(F32)
-    mine_at = p1 * 4 + p2
     dl[mine_at] = (part * (1.0 / 16.0)).astype(BF)
-
-    def plane(k):
-        return remote(
-            dl.at[mine_at], dl.at[mine_at], a_s.at[k - 1], a_r.at[k - 1], {"seq": s, "dp": z, "island": (isl + k) % 16}
-        )
 
     def share(k, carry):
         plane(k).start()
         return carry
 
     lax.fori_loop(1, 16, share, 0)
+    grads(48, 64)
+    ig_out(3).start()
 
     def arrived(k, carry):
         other = (isl + 16 - k) % 16
@@ -369,7 +445,7 @@
         return carry
 
     lax.fori_loop(1, 16, arrived, 0)
-    c_delta = pltpu.make_async_copy(dl, delta_hbm, outs.at[2])
+    c_delta = pltpu.make_async_copy(dl, delta_hbm, outs.at[5])
     c_delta.start()
 
     def drain(j, carry):
@@ -378,7 +454,7 @@
         return carry
 
     lax.fori_loop(0, EVENTS, drain, 0)
-    remote(own_x, other_x, pair_s.at[0], pair_r.at[0], partner).wait_send()
+    c_xs.wait_send()
     c_psel.wait_send()
 
     @pl.when(s == 0)
@@ -391,12 +467,12 @@
         c_mb1.wait_send()
 
     for k in range(1, 4):
-        remote(xs.at[0], xr.at[k - 1], xr_s.at[k - 1], xr_r.at[k - 1], first(k)).wait_send()
-        remote(ds16.at[0], dr16.at[k - 1], dr_s.at[k - 1], dr_r.at[k - 1], first(k)).wait_send()
-        remote(sall.at[0], sall.at[k], s_s.at[k - 1], s_r.at[k - 1], first(k)).wait_send()
-        remote(gs.at[0], r2.at[k - 1], p_s.at[k - 1], p_r.at[k - 1], second(k)).wait_send()
+        all_xr(k).wait_send()
+        send_dr(k).wait_send()
+        send_s(k).wait_send()
+        send_p(k).wait_send()
     for k in range(1, 8):
-        remote(t2b.at[0], r3.at[k - 1], z_s.at[k - 1], z_r.at[k - 1], along(k)).wait_send()
+        send_z(k).wait_send()
 
     def left_here(k, carry):
         plane(k).wait_send()
@@ -404,7 +480,8 @@
 
     lax.fori_loop(1, 16, left_here, 0)
     c_sg.wait()
-    c_ig.wait()
+    for c in range(4):
+        ig_out(c).wait()
     c_delta.wait()
 
 
@@ -460,9 +537,9 @@
             vm((T, 8192), BF),
             vm((T, 8192), BF),
             vm((8, 4, 128, 256), BF),
-            vm((4, 8, 256, 128), BF),
+            vm((256, 4096), BF),
             vm((3, 8, 256, 128), BF),
-            vm((8, 128, 1024), BF),
+            vm((1024, 1024), BF),
             vm((4, 128, 256), BF),
             vm((3, 128, 256), BF),
             vm((T, HEADS), F32),
@@ -477,8 +554,8 @@
             vm((3, T, T), F32),
             vm((2, 256, 256), BF),
             vm((2, 256, 256), BF),
-            vm((256, 256), F32),
-            vm((256, 256), F32),
+            vm((2, 256, T), F32),
+            vm((2, 256, T), F32),
             vm((256, 256), BF),
             vm((4, 256, 256), BF),
             vm((8, 128, 256), F32),
@@ -499,7 +576,7 @@
             dma((3,)), dma((3,)),
             dma((7,)), dma((7,)),
             dma((15,)), dma((15,)),
-            dma((3,)),
+            dma((6,)),
         ],
         compiler_params=pltpu.CompilerParams(
             collective_id=0, has_side_effects=True, vmem_limit_bytes=VMEM_LIMIT

time: 63.5 us -> 61.8 us (0.973)
  Pallas kernels: 62.7 us -> 60.4 us
    pallas_call x1, Pallas kernels: 59.5 us -> 57.1 us  [local(): pl.pallas_call(kernel, out_shape=(jax.ShapeDtypeStruct((T, 8192), BF), ja...]
where the time goes in v3:
time: 61.8 us; the launch traced here: 61.1 us
  Pallas kernels  60.4 us (98%)
  between operations  0.64 us (1%)
    pallas_call x1, Pallas kernels, local(): pl.pallas_call(kernel, out_shape=(jax.ShapeDtypeStruct((T, 8192), BF), ja...  57.1 us
    pallas_call x1, Pallas kernels, local(): pl.pallas_call(finish, out_shape=(jax.ShapeDtypeStruct((T, 8192), BF), ja...  3.28 us

profile of v3, /device:TPU:6, one launch (start us, length us, event | category | flops | bytes accessed | tf_op | source)
XLA Modules:
  0.0 61.1 jit_solution(8321341989707821852)
XLA Ops:
  0.6 57.1 %shard_map.102 = (bf16[128,8192]{1,0:T(8,128)(2,1)}, bf16[128,256]{1,0:T(8,128)(2,1)}, bf16[16,32,256]{2,1,0:T(8,128)(2,1)}) custom-call(bf16[128,8192]{1,0:T(8,128)(2,1)} %bitcast.7, bf16[128,8192]{1,0:T(8,128)(2,1)} %bitcast.8, bf16[128,8192]{1,0:T(8,128)(2,1)} %bitcast.9, f32[128,128]{1,0:T(8,128)} %bitcast.11, f32[512,256]{1,0:T(8,128)} %ow.1, ...), custom_call_target="tpu_custom_call" | custom-call | tf_op jit(solution)/shard_map/pallas_call | solution.py:524
  57.8 3.3 %shard_map.103 = (bf16[128,8192]{1,0:T(8,128)(2,1)}, bf16[128,256]{1,0:T(8,128)(2,1)}, f32[512,256]{1,0:T(8,128)}, f32[512,256]{1,0:T(8,128)}) custom-call(bf16[128,8192]{1,0:T(8,128)(2,1)} %get-tuple-element.11.ig, bf16[128,256]{1,0:T(8,128)(2,1)} %get-tuple-element.12.sg, bf16[16,32,256]{2,1,0:T(8,128)(2,1)} %get-tuple-element.13.dl, f32[512,256]{1,0:T(8,128)} %mo.1, ...), custom_call_target="tpu_custom_call" | custom-call | tf_op jit(solution)/shard_map/pallas_call | solution.py:587

commit v4 on v3

--- a/solution.py
+++ b/solution.py
@@ -62,17 +62,20 @@
 
     partner = {"seq": 1 - s, "dp": z, "island": isl}
 
-    barrier = pltpu.get_barrier_semaphore()
-    peers = [partner, along(1), along(7)] + [d(k) for d in (first, second) for k in (1, 2, 3)]
-    for d in peers:
-        pl.semaphore_signal(barrier, inc=1, device_id=d, device_id_type=MESH)
-
     c_ow = pltpu.make_async_copy(ow_hbm, ow, loc.at[0])
     c_dr = pltpu.make_async_copy(dr_hbm, dr, loc.at[1])
     c_dt = pltpu.make_async_copy(dt_hbm, dt, loc.at[2])
     c_ia = pltpu.make_async_copy(ia_hbm, ia, loc.at[3])
     c_dy = pltpu.make_async_copy(dy_hbm, dy, loc.at[4])
-    for c in (c_ow, c_dr, c_dt, c_dy, c_ia):
+    for c in (c_ow, c_dr):
+        c.start()
+
+    barrier = pltpu.get_barrier_semaphore()
+    peers = [partner, along(1), along(7)] + [d(k) for d in (first, second) for k in (1, 2, 3)]
+    for d in peers:
+        pl.semaphore_signal(barrier, inc=1, device_id=d, device_id_type=MESH)
+
+    for c in (c_dt, c_dy, c_ia):
         c.start()
 
     mine = pl.ds(pl.multiple_of(s * T, T), T)
@@ -250,11 +253,11 @@
     def busy(j, carry):
         event(j, j < 10)
         lax.fori_loop(3 * j - 18, 3 * j - 15, group_loop, 0)
-        return gain(j - 6, carry)
+        gain(2 * j - 12, carry)
+        return gain(2 * j - 11, carry)
 
     add(two_parts(z, 0, z, 1) + two_parts(z, 2, z, 3), True)
     lax.fori_loop(6, 11, busy, 0)
-    event(11, None)
     group(15)
 
     c_mb0 = remote(mb.at[pl.ds(0, 2)], mb.at[pl.ds(0, 2)], pair_s.at[3], pair_r.at[3], partner)
@@ -272,7 +275,8 @@
         mb[2] = mixacc[...]
         c_mb1.start()
 
-    lax.fori_loop(5, 12, gain, 0)
+    event(11, None)
+    lax.fori_loop(10, 12, gain, 0)
     event(12, None)
     gain(12, 0)
 
@@ -280,7 +284,6 @@
         xt[pl.ds(pl.multiple_of(zb * 128, 128), 128), 0:256] = xs[:, columns(zb, p1)].T
         return carry
 
-    lax.fori_loop(0, 8, turn_own, 0)
     @pl.when(s == 0)
     def _():
         c_mb1.wait_recv()
@@ -304,6 +307,7 @@
     gain(13, 0)
     c_psel = remote(psel, prem, pair_s.at[2], pair_r.at[2], partner)
     c_psel.start()
+    lax.fori_loop(0, 8, turn_own, 0)
 
     inv_root = 1.0 / math.sqrt(8192.0)
 
@@ -492,14 +496,14 @@
         pltpu.make_async_copy(ow, owv, ins.at[2]),
         pltpu.make_async_copy(sg, sgv, ins.at[3]),
     ]
-    parts = [pl.ds(2048 * c, 2048) for c in range(4)]
-    moves = [pltpu.make_async_copy(ig.at[:, p], igv.at[:, p], ins.at[4 + c]) for c, p in enumerate(parts)]
+    parts = [pl.ds(32 * c, 32) for c in range(4)]
+    moves = [pltpu.make_async_copy(ig.at[p], igv.at[p], ins.at[4 + c]) for c, p in enumerate(parts)]
     for c in loads + moves:
         c.start()
     ends = []
     for c, p in enumerate(parts):
         moves[c].wait()
-        ends.append(pltpu.make_async_copy(igv.at[:, p], ig_out.at[:, p], outs.at[4 + c]))
+        ends.append(pltpu.make_async_copy(igv.at[p], ig_out.at[p], outs.at[4 + c]))
         ends[c].start()
     for c in loads:
         c.wait()

time: 61.8 us -> 60.4 us (0.977); the launches traced: 61.1 us -> 60.3 us
  Pallas kernels: 60.4 us -> 59.7 us
    pallas_call x1, Pallas kernels: 57.1 us -> 56.4 us  [local(): pl.pallas_call(kernel, out_shape=(jax.ShapeDtypeStruct((T, 8192), BF), ja...]
where the time goes in v4:
time: 60.4 us; the launch traced here: 60.3 us
  Pallas kernels  59.7 us (99%)
  between operations  0.64 us (1%)
    pallas_call x1, Pallas kernels, local(): pl.pallas_call(kernel, out_shape=(jax.ShapeDtypeStruct((T, 8192), BF), ja...  56.4 us
    pallas_call x1, Pallas kernels, local(): pl.pallas_call(finish, out_shape=(jax.ShapeDtypeStruct((T, 8192), BF), ja...  3.28 us

profile of v4, /device:TPU:6, one launch (start us, length us, event | category | flops | bytes accessed | tf_op | source)
XLA Modules:
  0.0 60.3 jit_solution(16049790097877633607)
XLA Ops:
  0.6 56.4 %shard_map.102 = (bf16[128,8192]{1,0:T(8,128)(2,1)}, bf16[128,256]{1,0:T(8,128)(2,1)}, bf16[16,32,256]{2,1,0:T(8,128)(2,1)}) custom-call(bf16[128,8192]{1,0:T(8,128)(2,1)} %bitcast.7, bf16[128,8192]{1,0:T(8,128)(2,1)} %bitcast.8, bf16[128,8192]{1,0:T(8,128)(2,1)} %bitcast.9, f32[128,128]{1,0:T(8,128)} %bitcast.11, f32[512,256]{1,0:T(8,128)} %ow.1, ...), custom_call_target="tpu_custom_call" | custom-call | tf_op jit(solution)/shard_map/pallas_call | solution.py:528
  57.0 3.3 %shard_map.103 = (bf16[128,8192]{1,0:T(8,128)(2,1)}, bf16[128,256]{1,0:T(8,128)(2,1)}, f32[512,256]{1,0:T(8,128)}, f32[512,256]{1,0:T(8,128)}) custom-call(bf16[128,8192]{1,0:T(8,128)(2,1)} %get-tuple-element.11.ig, bf16[128,256]{1,0:T(8,128)(2,1)} %get-tuple-element.12.sg, bf16[16,32,256]{2,1,0:T(8,128)(2,1)} %get-tuple-element.13.dl, f32[512,256]{1,0:T(8,128)} %mo.1, ...), custom_call_target="tpu_custom_call" | custom-call | tf_op jit(solution)/shard_map/pallas_call | solution.py:591

commit v5 on v4

--- a/solution.py
+++ b/solution.py
@@ -423,7 +423,7 @@
 
     def plane(k):
         at = dl.at[mine_at]
-        device = {"seq": s, "dp": z, "island": (isl + k) % 16}
+        device = {"seq": s, "dp": z, "island": (y + k // 4) % 4 * 4 + (x + k % 4) % 4}
         return remote(at, at, a_s.at[k - 1], a_r.at[k - 1], device)
 
     part = t2[z]
@@ -432,25 +432,10 @@
         part = part + r3[k - 1].astype(F32)
     dl[mine_at] = (part * (1.0 / 16.0)).astype(BF)
 
-    def share(k, carry):
+    for k in sorted(range(1, 16), key=lambda k: -(min(k // 4, 4 - k // 4) + min(k % 4, 4 - k % 4))):
         plane(k).start()
-        return carry
-
-    lax.fori_loop(1, 16, share, 0)
     grads(48, 64)
     ig_out(3).start()
-
-    def arrived(k, carry):
-        other = (isl + 16 - k) % 16
-        oy = other // 4
-        ox = other % 4
-        at = dl.at[(ox + s * (oy - ox)) * 4 + oy + s * (ox - oy)]
-        remote(at, at, a_s.at[k - 1], a_r.at[k - 1], partner).wait_recv()
-        return carry
-
-    lax.fori_loop(1, 16, arrived, 0)
-    c_delta = pltpu.make_async_copy(dl, delta_hbm, outs.at[5])
-    c_delta.start()
 
     def drain(j, carry):
         right(j, z, 0).wait_send()
@@ -477,6 +462,17 @@
         send_p(k).wait_send()
     for k in range(1, 8):
         send_z(k).wait_send()
+
+    def arrived(k, carry):
+        oy = (y + 4 - k // 4) % 4
+        ox = (x + 4 - k % 4) % 4
+        at = dl.at[(ox + s * (oy - ox)) * 4 + oy + s * (ox - oy)]
+        remote(at, at, a_s.at[k - 1], a_r.at[k - 1], partner).wait_recv()
+        return carry
+
+    lax.fori_loop(1, 16, arrived, 0)
+    c_delta = pltpu.make_async_copy(dl, delta_hbm, outs.at[5])
+    c_delta.start()
 
     def left_here(k, carry):
         plane(k).wait_send()

time: 60.4 us -> 60.2 us (level)
  no operation moved by 1% of the time
where the time goes in v5:
time: 60.2 us; the launch traced here: 59.8 us
  Pallas kernels  59.2 us (98%)
  between operations  0.64 us (1%)
    pallas_call x1, Pallas kernels, local(): pl.pallas_call(kernel, out_shape=(jax.ShapeDtypeStruct((T, 8192), BF), ja...  55.9 us
    pallas_call x1, Pallas kernels, local(): pl.pallas_call(finish, out_shape=(jax.ShapeDtypeStruct((T, 8192), BF), ja...  3.28 us

profile of v5, /device:TPU:6, one launch (start us, length us, event | category | flops | bytes accessed | tf_op | source)
XLA Modules:
  0.0 59.8 jit_solution(7373268117405838831)
XLA Ops:
  0.6 55.9 %shard_map.102 = (bf16[128,8192]{1,0:T(8,128)(2,1)}, bf16[128,256]{1,0:T(8,128)(2,1)}, bf16[16,32,256]{2,1,0:T(8,128)(2,1)}) custom-call(bf16[128,8192]{1,0:T(8,128)(2,1)} %bitcast.7, bf16[128,8192]{1,0:T(8,128)(2,1)} %bitcast.8, bf16[128,8192]{1,0:T(8,128)(2,1)} %bitcast.9, f32[128,128]{1,0:T(8,128)} %bitcast.11, f32[512,256]{1,0:T(8,128)} %ow.1, ...), custom_call_target="tpu_custom_call" | custom-call | tf_op jit(solution)/shard_map/pallas_call | solution.py:524
  56.5 3.3 %shard_map.103 = (bf16[128,8192]{1,0:T(8,128)(2,1)}, bf16[128,256]{1,0:T(8,128)(2,1)}, f32[512,256]{1,0:T(8,128)}, f32[512,256]{1,0:T(8,128)}) custom-call(bf16[128,8192]{1,0:T(8,128)(2,1)} %get-tuple-element.11.ig, bf16[128,256]{1,0:T(8,128)(2,1)} %get-tuple-element.12.sg, bf16[16,32,256]{2,1,0:T(8,128)(2,1)} %get-tuple-element.13.dl, f32[512,256]{1,0:T(8,128)} %mo.1, ...), custom_call_target="tpu_custom_call" | custom-call | tf_op jit(solution)/shard_map/pallas_call | solution.py:587
